TPU v7x, 256 devices: a whole 4x4x8 slice. The times are simulated.
256 devices in a mesh: row: 32 (over x_hi, z, core), blk: 8 (over y, x_lo).
Axes of the slice: x: 4 (x_hi: 2, x_lo: 2; x = x_hi * 2 + x_lo), y: 4, z: 8, core: 2. Of those that a mesh axis runs over, the one named last changes fastest.
Arguments:
- features: bfloat16 [98304, 256], P(('row', 'blk')), may hold values from -6 to 6
- adj_tiles: bfloat16 [32, 2304, 128, 128], P('row', 'blk'), may hold values from -0.15625 to 0.15625
- tile_row: int32 [32, 2304], P('row', 'blk'), may hold values from 0 to 23, as said below
- tile_col: int32 [32, 2304], P('row', 'blk'), may hold values from 0 to 96, as said below
- weight: bfloat16 [256, 256], replicated, may hold values from -0.375 to 0.375
- bias_vec: float32 [256], replicated, may hold values from -3 to 3
- cotangent: bfloat16 [98304, 256], P(('row', 'blk')), may hold values from -6 to 6
Outputs:
- activated: bfloat16 [98304, 256], P(('row', 'blk'))
- grad_x: bfloat16 [98304, 256], P(('row', 'blk'))
- grad_w: float32 [256, 256], replicated
- grad_b: float32 [256], replicated
Inputs may be any that keep to these rules, and one draw needn't show every extreme that they name: On each device the 288 slots of tile_col are non-decreasing; live slots hold 0 to 95 and come first, dead slots hold 96; live (tile_row, tile_col) pairs on one device are distinct; a device has 72 to 288 live slots, and at least one device has 288. `tile_row`: dead slots hold 0.
All inputs are finite; a program needn't handle non-finite values.
Results may differ from a plain program's by a relative error of at most 0.0075.
Values may be sent and summed in bfloat16 or wider, within the bound.
No kernel may reach another device: no remote copies, remote signals or barrier semaphores. Data moves between devices by JAX's collectives and lax.ppermute only.
A program may use at most 128 MiB of HBM per device.

v0:
```python
import functools
import math

import jax
import jax.numpy as jnp
from jax import lax
from jax.experimental import pallas as pl
from jax.experimental.pallas import tpu as pltpu
from jax.sharding import Mesh, PartitionSpec as P

XH, Z, CORE, Y, XL = 2, 8, 2, 4, 2
AXES = ("xh", "z", "core", "y", "xl")
BLK = ("y", "xl")
N_BLK = Y * XL
TILE = 128
HIDDEN = 256
PER = 3
NB = PER * TILE
TR = N_BLK * PER
TC = XH * Z * CORE * PER
K = 288
GROUP = 16
GROUPS = K // GROUP
EXTRA = 48
GRAD_ROWS = HIDDEN // N_BLK
CHAIN = Z // 2 * XH * PER
VMEM_BYTES = 56 * 2**20
bf16 = jnp.bfloat16
f32 = jnp.float32

TILE_COST = pl.CostEstimate(
    flops=2 * K * TILE * TILE * HIDDEN, bytes_accessed=6 * K * TILE * TILE, transcendentals=0
)
ANY = pl.BlockSpec(memory_space=pl.ANY)
VMEM = pl.BlockSpec(memory_space=pltpu.VMEM)


def swap(axis):
    return lambda v: lax.ppermute(v, axis, [(0, 1), (1, 0)])


def turn(v, step):
    return lax.ppermute(v, "z", [(i, (i + step) % Z) for i in range(Z)])


def fetch_group(live, adj_hbm, adj, sem, g):
    first = jnp.minimum(g * GROUP, K - GROUP)
    return pltpu.make_async_copy(adj_hbm.at[pl.ds(first, GROUP)], adj.at[g], sem.at[g])


def start_groups(live_ref, adj_hbm, adj, sem):
    live = live_ref[0]
    groups = (live + GROUP - 1) // GROUP

    def begin(g, carry):
        fetch_group(live, adj_hbm, adj, sem, g).start()
        return carry

    lax.fori_loop(0, groups, begin, 0)
    return live, groups


def forward_kernel(live_ref, row_ref, pos_ref, adj_hbm, *refs):
    pieces = refs[:-6]
    out_ref, adj, slab, acc, adj_sem, piece_sem = refs[-6:]
    copies = []
    at = 0
    for n, piece in enumerate(pieces):
        size = piece.shape[0]
        copies.append(pltpu.make_async_copy(piece, slab.at[pl.ds(at, size)], piece_sem.at[n]))
        at += size
    for copy in copies:
        copy.start()
    live, groups = start_groups(live_ref, adj_hbm, adj, adj_sem)
    acc[...] = jnp.zeros_like(acc)
    for copy in copies:
        copy.wait()

    def step(g, carry):
        fetch_group(live, adj_hbm, adj, adj_sem, g).wait()
        for u in range(GROUP):
            k = g * GROUP + u
            row = jnp.where(k < live, row_ref[k], TR)
            acc[row] += jnp.dot(adj[g, u], slab[pos_ref[k]], preferred_element_type=f32)
        return carry

    lax.fori_loop(0, groups, step, 0)
    out_ref[...] = acc[:TR].astype(bf16)


def forward_tiles(live, rows, pos, adj, pieces):
    return pl.pallas_call(
        forward_kernel,
        out_shape=jax.ShapeDtypeStruct((TR, TILE, HIDDEN), bf16),
        grid_spec=pltpu.PrefetchScalarGridSpec(
            num_scalar_prefetch=3,
            grid=(),
            in_specs=[ANY] * (1 + len(pieces)),
            out_specs=VMEM,
            scratch_shapes=[
                pltpu.VMEM((GROUPS, GROUP, TILE, TILE), bf16),
                pltpu.VMEM((TC, TILE, HIDDEN), bf16),
                pltpu.VMEM((TR + 1, TILE, HIDDEN), f32),
                pltpu.SemaphoreType.DMA((GROUPS,)),
                pltpu.SemaphoreType.DMA((len(pieces),)),
            ],
        ),
        compiler_params=pltpu.CompilerParams(vmem_limit_bytes=VMEM_BYTES),
        cost_estimate=TILE_COST,
        name="forward_tiles",
    )(live, rows, pos, adj, *pieces)


def backward_kernel(live_ref, row_ref, pos_ref, adj_hbm, err_hbm, *refs):
    outs = refs[:-5]
    adj, err, acc, adj_sem, err_sem = refs[-5:]
    copies = [
        pltpu.make_async_copy(
            err_hbm.at[i // PER, pl.ds(i % PER * TILE, TILE)], err.at[i], err_sem.at[i]
        )
        for i in range(TR)
    ]
    for copy in copies:
        copy.start()
    live, groups = start_groups(live_ref, adj_hbm, adj, adj_sem)
    acc[...] = jnp.zeros_like(acc)
    for copy in copies:
        copy.wait()

    def step(g, carry):
        fetch_group(live, adj_hbm, adj, adj_sem, g).wait()
        for u in range(GROUP):
            k = g * GROUP + u
            pos = jnp.where(k < live, pos_ref[k], TC)
            acc[pos] += lax.dot_general(
                adj[g, u], err[row_ref[k]], (((0,), (0,)), ((), ())), preferred_element_type=f32
            )
        return carry

    lax.fori_loop(0, groups, step, 0)
    for i, out in enumerate(outs):
        out[...] = acc[i * CHAIN : (i + 1) * CHAIN].astype(bf16)


def backward_tiles(live, rows, pos, adj, err):
    return pl.pallas_call(
        backward_kernel,
        out_shape=[jax.ShapeDtypeStruct((CHAIN, TILE, HIDDEN), bf16)] * (TC // CHAIN),
        grid_spec=pltpu.PrefetchScalarGridSpec(
            num_scalar_prefetch=3,
            grid=(),
            in_specs=[ANY, ANY],
            out_specs=[VMEM] * (TC // CHAIN),
            scratch_shapes=[
                pltpu.VMEM((GROUPS, GROUP, TILE, TILE), bf16),
                pltpu.VMEM((TR, TILE, HIDDEN), bf16),
                pltpu.VMEM((TC + 1, TILE, HIDDEN), f32),
                pltpu.SemaphoreType.DMA((GROUPS,)),
                pltpu.SemaphoreType.DMA((TR,)),
            ],
        ),
        compiler_params=pltpu.CompilerParams(vmem_limit_bytes=VMEM_BYTES),
        cost_estimate=TILE_COST,
        name="backward_tiles",
    )(live, rows, pos, adj, err)


def dense_kernel(scale, parts_ref, weight_ref, bias_ref, cot_ref, act_ref, back_ref):
    summed = parts_ref[0].astype(f32)
    for b in range(1, N_BLK):
        summed = summed + parts_ref[b].astype(f32)
    agg = summed.astype(bf16)
    weight = weight_ref[...]
    v = jnp.dot(agg, weight, preferred_element_type=f32) + bias_ref[...]
    c = math.sqrt(2.0 / math.pi)
    t = jnp.tanh(c * (v + 0.044715 * (v * v * v)))
    act_ref[...] = (0.5 * v * (1.0 + t)).astype(bf16)
    slope = 0.5 * (1.0 + t) + 0.5 * v * (1.0 - t * t) * (c * (1.0 + 3.0 * 0.044715 * (v * v)))
    delta = (cot_ref[...].astype(f32) * slope).astype(bf16)
    back = lax.dot_general(
        delta, weight, (((1,), (1,)), ((), ())), preferred_element_type=f32
    ).astype(bf16)
    over_nodes = (((0,), (0,)), ((), ()))
    grad_w = lax.dot_general(agg, delta, over_nodes, preferred_element_type=f32) * scale
    grad_b = jnp.sum(delta.astype(f32), axis=0, keepdims=True) * scale
    grad_b = jnp.broadcast_to(grad_b, (EXTRA - GRAD_ROWS, HIDDEN)).astype(bf16)
    for b in range(N_BLK):
        back_ref[b, :NB] = back
        back_ref[b, NB : NB + GRAD_ROWS] = grad_w[b * GRAD_ROWS : (b + 1) * GRAD_ROWS].astype(bf16)
        back_ref[b, NB + GRAD_ROWS :] = grad_b


def dense_block(parts, weight, bias, cot, scale):
    return pl.pallas_call(
        functools.partial(dense_kernel, scale),
        out_shape=[
            jax.ShapeDtypeStruct((NB, HIDDEN), bf16),
            jax.ShapeDtypeStruct((N_BLK, NB + EXTRA, HIDDEN), bf16),
        ],
        in_specs=[VMEM] * 4,
        out_specs=[VMEM] * 2,
        compiler_params=pltpu.CompilerParams(vmem_limit_bytes=VMEM_BYTES),
        name="dense_block",
    )(parts, weight, bias, cot)


def gather_pieces(own):
    here, across = own, swap("xh")(own)
    near = [(here, across)]
    right = left = near[0]
    for _ in range(3):
        right = tuple(turn(v, 1) for v in right)
        left = tuple(turn(v, -1) for v in left)
        near += [right, left]
    near.append((turn(right[0], 1), turn(left[1], -1)))
    pieces = []
    for pair in near:
        pieces += [*pair, *(swap("core")(v) for v in pair)]
    return pieces


def place_of(cols, xh, z, core):
    owner = cols // PER
    away = ((owner // CORE) % Z - z) % Z
    near = jnp.where(away <= 3, 2 * away, 15 - 2 * away)
    return near, (owner % CORE) ^ core, (owner // (CORE * Z)) ^ xh, cols % PER


def scatter_sum(keep, sends):
    odd = swap("core")(sends[1])
    received = [swap("core")(sends[0]), odd]

    def mine(near):
        at = slice(near // 2 * XH * PER, (near // 2 + 1) * XH * PER)
        return keep[near % 2][at].astype(f32) + received[near % 2][at].astype(f32)

    far = mine(7).astype(bf16)
    right, left = turn(far[:PER], 1), turn(far[PER:], -1)
    first = right[0, :EXTRA].astype(f32) + left[0, :EXTRA].astype(f32)
    onto_right, onto_left = mine(6), mine(5)
    right = jnp.concatenate([onto_right[:PER] + right.astype(f32), onto_right[PER:]], axis=0)
    left = jnp.concatenate([onto_left[:PER], onto_left[PER:] + left.astype(f32)], axis=0)
    for near in (4, 2):
        right, left = turn(right.astype(bf16), 1), turn(left.astype(bf16), -1)
        third = right[0, :EXTRA].astype(f32) + left[0, :EXTRA].astype(f32)
        right = mine(near) + right.astype(f32)
        left = mine(near - 1) + left.astype(f32)
    here = mine(0) + turn(right.astype(bf16), 1).astype(f32) + turn(left.astype(bf16), -1).astype(f32)
    across = swap("xh")(here[PER:].astype(bf16))
    return (here[:PER] + across.astype(f32)).astype(bf16), first, third


def both_sides(rows, axis):
    rows = rows.astype(bf16)
    return rows.astype(f32) + swap(axis)(rows).astype(f32)


def shards(features, adj_tiles, tile_row, tile_col, weight, bias_vec, cotangent):
    adj = adj_tiles[0]
    rows = tile_row[0]
    cols = tile_col[0]
    xh, z, core = (lax.axis_index(axis) for axis in ("xh", "z", "core"))
    live = jnp.sum((cols < TC).astype(jnp.int32)).reshape(1)
    near, other, across, part = place_of(jnp.minimum(cols, TC - 1), xh, z, core)
    slab_pos = ((near * CORE + other) * XH + across) * PER + part
    sum_pos = (((other * 2 + near % 2) * (Z // 2) + near // 2) * XH + across) * PER + part

    pieces = gather_pieces(features.reshape(PER, TILE, HIDDEN))
    partial = forward_tiles(live, rows, slab_pos, adj, pieces)
    parts = lax.all_to_all(
        partial.reshape(N_BLK, NB, HIDDEN), BLK, split_axis=0, concat_axis=0, tiled=True
    )
    scale = 1.0 / math.sqrt(NB * XH * Z * CORE * N_BLK)
    activated, back = dense_block(parts, weight, bias_vec.reshape(1, HIDDEN), cotangent, scale)
    back = lax.all_to_all(back, BLK, split_axis=0, concat_axis=0, tiled=True)

    outs = backward_tiles(live, rows, sum_pos, adj, back)
    grad_x, first, third = scatter_sum(outs[:2], outs[2:])

    grads = jnp.sum(back[:, NB:].astype(f32), axis=0)
    grads = both_sides(both_sides(grads, "core"), "xh")
    grads = (grads + 0.0 * first).astype(bf16)
    by_z = lax.all_to_all(jnp.tile(grads, (Z, 1)), "z", split_axis=0, concat_axis=0, tiled=True)
    grads = jnp.sum(by_z.reshape(Z, EXTRA, HIDDEN).astype(f32), axis=0)
    grads = grads + 0.0 * third
    grad_w = lax.all_to_all(
        jnp.tile(grads[:GRAD_ROWS], (N_BLK, 1)), BLK, split_axis=0, concat_axis=0, tiled=True
    )
    return (activated, grad_x.reshape(NB, HIDDEN), grad_w, grads[GRAD_ROWS])


def solution(mesh):
    cut = Mesh(mesh.devices.reshape(XH, Z, CORE, Y, XL), AXES)
    row = ("xh", "z", "core")
    return jax.shard_map(
        shards,
        mesh=cut,
        in_specs=(
            P(AXES, None),
            P(row, BLK, None, None),
            P(row, BLK),
            P(row, BLK),
            P(),
            P(),
            P(AXES, None),
        ),
        out_specs=(P(AXES, None), P(AXES, None), P(), P()),
        check_vma=False,
    )
```

profile of v0, /device:TPU:2, one launch (start us, length us, event | category | flops | bytes accessed | tf_op | source)
XLA Modules:
  0.0 198.7 jit_solution(6780456342499643754)
XLA Ops:
  0.6 5.9 %collective-permute-start.7 = (bf16[3,128,256]{2,1,0:T(8,128)(2,1)}, bf16[3,128,256]{2,1,0:T(8,128)(2,1)S(1)}, u32[]{:S(2)}, u32[]{:S(2)}) collective-permute-start(bf16[3,128,256]{2,1,0:T(8,128)(2,1)} %bitcast.18), channel_id=1, source_target_pairs={{0,112},{16,0},{32,16},{48,32},{64,48},{80,64},{96,80},{112,96},{1... | collective-permute-start | bytes 589832 | tf_op jit(solution)/shard_map/ppermute | solution.py:43
  6.6 2.1 %collective-permute-start = (bf16[3,128,256]{2,1,0:T(8,128)(2,1)}, bf16[3,128,256]{2,1,0:T(8,128)(2,1)S(1)}, u32[]{:S(2)}, u32[]{:S(2)}) collective-permute-start(bf16[3,128,256]{2,1,0:T(8,128)(2,1)} %bitcast.21), channel_id=1, source_target_pairs={{0,128},{128,0},{1,129},{129,1},{2,130},{130,2},{3,131},{131,3},{4... | collective-permute-start | bytes 589832 | tf_op jit(solution)/shard_map/ppermute | solution.py:39
  8.7 2.3 %collective-permute-done.7.refs_8_ = bf16[3,128,256]{2,1,0:T(8,128)(2,1)S(1)} collective-permute-done((bf16[3,128,256]{2,1,0:T(8,128)(2,1)}, bf16[3,128,256]{2,1,0:T(8,128)(2,1)S(1)}, u32[]{:S(2)}, u32[]{:S(2)}) %collective-permute-start.7) | collective-permute-done | bytes 196640 | tf_op jit(solution)/shard_map/ppermute | solution.py:43
  11.0 3.6 %collective-permute-start.15 = (bf16[3,128,256]{2,1,0:T(8,128)(2,1)S(1)}, bf16[3,128,256]{2,1,0:T(8,128)(2,1)S(1)}, u32[]{:S(2)}, u32[]{:S(2)}) collective-permute-start(bf16[3,128,256]{2,1,0:T(8,128)(2,1)S(1)} %collective-permute-done.7.refs_8_), channel_id=1, source_target_pairs={{0,112},{16,0},{32,16},{48,32},{64,48},{80,64},{96,80},{112,96},{1... | collective-permute-start | bytes 589832 | tf_op jit(solution)/shard_map/ppermute | solution.py:43
  14.8 0.5 collective-permute-start.5
  15.3 0.3 collective-permute-done.refs_1_
  15.6 3.2 %collective-permute-start.8 = (bf16[3,128,256]{2,1,0:T(8,128)(2,1)S(1)}, bf16[3,128,256]{2,1,0:T(8,128)(2,1)S(1)}, u32[]{:S(2)}, u32[]{:S(2)}) collective-permute-start(bf16[3,128,256]{2,1,0:T(8,128)(2,1)S(1)} %collective-permute-done.refs_1_), channel_id=1, source_target_pairs={{0,112},{16,0},{32,16},{48,32},{64,48},{80,64},{96,80},{112,96},{1... | collective-permute-start | bytes 589832 | tf_op jit(solution)/shard_map/ppermute | solution.py:43
  19.0 4.7 %collective-permute-done.11.refs_12_ = bf16[3,128,256]{2,1,0:T(8,128)(2,1)S(1)} collective-permute-done((bf16[3,128,256]{2,1,0:T(8,128)(2,1)S(1)}, bf16[3,128,256]{2,1,0:T(8,128)(2,1)S(1)}, u32[]{:S(2)}, u32[]{:S(2)}) %collective-permute-start.11) | collective-permute-done | bytes 196640 | tf_op jit(solution)/shard_map/ppermute | solution.py:43
  23.8 2.0 %collective-permute-start.19 = (bf16[3,128,256]{2,1,0:T(8,128)(2,1)S(1)}, bf16[3,128,256]{2,1,0:T(8,128)(2,1)S(1)}, u32[]{:S(2)}, u32[]{:S(2)}) collective-permute-start(bf16[3,128,256]{2,1,0:T(8,128)(2,1)S(1)} %collective-permute-done.11.refs_12_), channel_id=1, source_target_pairs={{0,16},{16,32},{32,48},{48,64},{64,80},{80,96},{96,112},{112,0},{1... | collective-permute-start | bytes 589832 | tf_op jit(solution)/shard_map/ppermute | solution.py:43
  25.8 1.6 collective-permute-done.4.refs_5_
  27.5 1.3 reduce.2.row_ref
  28.8 0.8 collective-permute-done.23.refs_24_
  29.7 1.3 collective-permute-start.12
  31.0 1.3 collective-permute-done.19.refs_20_
  32.3 0.5 collective-permute-start.25
  32.8 1.9 collective-permute-done.16.refs_17_
  34.7 1.5 collective-permute-start.24
  36.2 0.7 compare_reduce_fusion
  36.9 1.3 remainder_reduce_fusion
  38.3 0.5 collective-permute-start.27
  38.8 0.5 collective-permute-start.18
  39.4 1.7 collective-permute-done.24.refs_25_
  41.2 2.9 %collective-permute-start.28 = (bf16[3,128,256]{2,1,0:T(8,128)(2,1)S(1)}, bf16[3,128,256]{2,1,0:T(8,128)(2,1)S(1)}, u32[]{:S(2)}, u32[]{:S(2)}) collective-permute-start(bf16[3,128,256]{2,1,0:T(8,128)(2,1)S(1)} %collective-permute-done.24.refs_25_), channel_id=1, source_target_pairs={{0,112},{16,0},{32,16},{48,32},{64,48},{80,64},{96,80},{112,96},{1... | collective-permute-start | bytes 589832 | tf_op jit(solution)/shard_map/ppermute | solution.py:43
  44.1 0.6 fusion.16
  44.7 2.6 %collective-permute-done.27.refs_28_ = bf16[3,128,256]{2,1,0:T(8,128)(2,1)S(1)} collective-permute-done((bf16[3,128,256]{2,1,0:T(8,128)(2,1)S(1)}, bf16[3,128,256]{2,1,0:T(8,128)(2,1)S(1)}, u32[]{:S(2)}, u32[]{:S(2)}) %collective-permute-start.27) | collective-permute-done | bytes 196640 | tf_op jit(solution)/shard_map/ppermute | solution.py:43
  47.3 0.5 collective-permute-start.26
  47.9 2.1 %collective-permute-done.20.refs_21_ = bf16[3,128,256]{2,1,0:T(8,128)(2,1)S(1)} collective-permute-done((bf16[3,128,256]{2,1,0:T(8,128)(2,1)S(1)}, bf16[3,128,256]{2,1,0:T(8,128)(2,1)S(1)}, u32[]{:S(2)}, u32[]{:S(2)}) %collective-permute-start.20) | collective-permute-done | bytes 196640 | tf_op jit(solution)/shard_map/ppermute | solution.py:43
  50.1 0.5 collective-permute-start.30
  50.6 0.6 multiply_add_fusion.pos_ref
  52.1 0.3 copy-done.33
  52.4 10.1 %forward_tiles.1 = bf16[24,128,256]{2,1,0:T(8,128)(2,1)} custom-call(s32[1]{0:T(128)} %bitcast.live_ref, s32[288]{0:T(512)} %reduce.2.row_ref, s32[288]{0:T(512)} %multiply_add_fusion.pos_ref, bf16[288,128,128]{2,1,0:T(8,128)(2,1)} %bitcast.14, bf16[3,128,256]{2,1,0:T(8,128)(2,1)} %bitcast.22, bf16[3,128,256]{2,1,0:T(8,128)(2,1)} %copy-done.6, ...), custom_call_target="tpu_custom_call" | custom-call | flops 2415919104 | bytes 28311552 | tf_op jit(solution)/shard_map/forward_tiles/pallas_call | solution.py:92
  62.6 25.9 %all_to_all.25.parts_ref = bf16[8,384,256]{2,1,0:T(8,128)(2,1)} all-to-all(bf16[8,384,256]{2,1,0:T(8,128)(2,1)} %bitcast.16), channel_id=1, replica_groups=mesh['xh'=2,'z'=8,'core'=2,'y'=4,'xl'=2] {'y','xl'}, dimensions={0} | all-to-all | bytes 3145728 | tf_op jit(solution)/shard_map/all_to_all | solution.py:270
  88.5 3.5 %dense_block.1 = (bf16[384,256]{1,0:T(8,128)(2,1)}, bf16[8,432,256]{2,1,0:T(8,128)(2,1)}) custom-call(bf16[8,384,256]{2,1,0:T(8,128)(2,1)} %all_to_all.25.parts_ref, bf16[256,256]{1,0:T(8,128)(2,1)} %weight_ref.1, f32[1,256]{1,0:T(1,128)} %bitcast.24, bf16[384,256]{1,0:T(8,128)(2,1)} %cot_ref.1), custom_call_target="tpu_custom_call" | custom-call | tf_op jit(solution)/shard_map/dense_block/pallas_call | solution.py:194
  92.0 28.9 %all_to_all.26.err_hbm = bf16[8,432,256]{2,1,0:T(8,128)(2,1)} all-to-all(bf16[8,432,256]{2,1,0:T(8,128)(2,1)} %get-tuple-element.11), channel_id=1, replica_groups=mesh['xh'=2,'z'=8,'core'=2,'y'=4,'xl'=2] {'y','xl'}, dimensions={0} | all-to-all | bytes 3538944 | tf_op jit(solution)/shard_map/all_to_all | solution.py:275
  120.9 10.7 %backward_tiles.1 = (bf16[24,128,256]{2,1,0:T(8,128)(2,1)}, bf16[24,128,256]{2,1,0:T(8,128)(2,1)}, bf16[24,128,256]{2,1,0:T(8,128)(2,1)}, bf16[24,128,256]{2,1,0:T(8,128)(2,1)}) custom-call(s32[1]{0:T(128)} %bitcast.live_ref, s32[288]{0:T(512)} %reduce.2.row_ref, s32[288]{0:T(512)} %get-tuple-element.19.pos_ref, bf16[288,128,128]{2,1,0:T(8,128)(2,1)} %bitcast.15, ...), custom_call_target="tpu_custom_call" | custom-call | flops 2415919104 | bytes 28311552 | tf_op jit(solution)/shard_map/backward_tiles/pallas_call | solution.py:146
  131.7 0.5 collective-permute-start.31
  132.2 1.0 slice_reduce_fusion
  133.3 2.0 collective-permute-done.32
  135.3 1.9 add_convert_fusion.4
  137.3 0.8 collective-permute-start.37
  138.2 1.4 collective-permute-start.33
  139.6 4.7 %collective-permute-done.37 = bf16[3,128,256]{2,1,0:T(8,128)(2,1)S(1)} collective-permute-done((bf16[3,128,256]{2,1,0:T(8,128)(2,1)S(1)}, bf16[3,128,256]{2,1,0:T(8,128)(2,1)S(1)}, u32[]{:S(2)}, u32[]{:S(2)}) %collective-permute-start.37) | collective-permute-done | bytes 196640 | tf_op jit(solution)/shard_map/ppermute | solution.py:43
  144.4 2.0 %collective-permute-start.38 = (bf16[6,128,256]{2,1,0:T(8,128)(2,1)S(1)}, bf16[6,128,256]{2,1,0:T(8,128)(2,1)S(1)}, u32[]{:S(2)}, u32[]{:S(2)}) collective-permute-start(bf16[6,128,256]{2,1,0:T(8,128)(2,1)S(1)} %pad_maximum_fusion.1), channel_id=1, source_target_pairs={{0,112},{16,0},{32,16},{48,32},{64,48},{80,64},{96,80},{112,96},{1... | collective-permute-start | bytes 1179656 | tf_op jit(solution)/shard_map/ppermute | solution.py:43
  146.7 5.3 %collective-permute-start.43 = (bf16[48,256]{1,0:T(8,128)(2,1)S(1)}, bf16[48,256]{1,0:T(8,128)(2,1)S(1)}, u32[]{:S(2)}, u32[]{:S(2)}) collective-permute-start(bf16[48,256]{1,0:T(8,128)(2,1)S(1)} %add_convert_fusion.5), channel_id=1, source_target_pairs={{0,128},{128,0},{1,129},{129,1},{2,130},{130,2},{3,131},{131,3},{4... | collective-permute-start | bytes 73736 | tf_op jit(solution)/shard_map/ppermute | solution.py:39
  152.0 2.8 %collective-permute-done.38 = bf16[6,128,256]{2,1,0:T(8,128)(2,1)S(1)} collective-permute-done((bf16[6,128,256]{2,1,0:T(8,128)(2,1)S(1)}, bf16[6,128,256]{2,1,0:T(8,128)(2,1)S(1)}, u32[]{:S(2)}, u32[]{:S(2)}) %collective-permute-start.38) | collective-permute-done | bytes 393248 | tf_op jit(solution)/shard_map/ppermute | solution.py:43
  154.8 1.9 add_convert_fusion.1
  156.7 3.2 %collective-permute-start.39 = (bf16[6,128,256]{2,1,0:T(8,128)(2,1)}, bf16[6,128,256]{2,1,0:T(8,128)(2,1)}, u32[]{:S(2)}, u32[]{:S(2)}) collective-permute-start(bf16[6,128,256]{2,1,0:T(8,128)(2,1)} %add_convert_fusion.1), channel_id=1, source_target_pairs={{0,112},{16,0},{32,16},{48,32},{64,48},{80,64},{96,80},{112,96},{1... | collective-permute-start | bytes 1179656 | tf_op jit(solution)/shard_map/ppermute | solution.py:43
  159.9 0.9 add_convert_fusion.3
  160.8 0.7 tile.4
  161.5 6.4 %all-to-all-start.2 = ((bf16[8,48,256]{2,1,0:T(8,128)(2,1)}), bf16[8,48,256]{2,1,0:T(8,128)(2,1)S(1)}, u32[]{:S(2)}, u32[]{:S(2)}) async-start(bf16[8,48,256]{2,1,0:T(8,128)(2,1)} %tile.4), calls=%async_computation.2 | async-start | bytes 393216 | tf_op jit(solution)/shard_map/all_to_all | solution.py:283
  167.9 2.1 %add_convert_fusion = bf16[6,128,256]{2,1,0:T(8,128)(2,1)} fusion(bf16[6,128,256]{2,1,0:T(8,128)(2,1)} %collective-permute-done.39, bf16[24,128,256]{2,1,0:T(8,128)(2,1)} %copy-done.2, bf16[24,128,256]{2,1,0:T(8,128)(2,1)} %get-tuple-element.14), kind=kLoop, calls=%fused_computation.1 | loop fusion | flops 1179648 | bytes 1572864 | tf_op jit(solution)/shard_map/convert_element_type | solution.py:248
  170.1 3.2 %collective-permute-start.40 = (bf16[6,128,256]{2,1,0:T(8,128)(2,1)}, bf16[6,128,256]{2,1,0:T(8,128)(2,1)}, u32[]{:S(2)}, u32[]{:S(2)}) collective-permute-start(bf16[6,128,256]{2,1,0:T(8,128)(2,1)} %add_convert_fusion), channel_id=1, source_target_pairs={{0,112},{16,0},{32,16},{48,32},{64,48},{80,64},{96,80},{112,96},{1... | collective-permute-start | bytes 1179656 | tf_op jit(solution)/shard_map/ppermute | solution.py:43
  173.3 1.9 add_convert_fusion.2
  175.2 1.8 all-to-all-done.2
  177.0 0.8 bitcast_add_fusion
  177.8 0.7 tile.5
  178.5 10.1 %all-to-all-start.3 = ((f32[8,32,256]{2,1,0:T(8,128)}), f32[8,32,256]{2,1,0:T(8,128)S(1)}, u32[]{:S(2)}, u32[]{:S(2)}) async-start(f32[8,32,256]{2,1,0:T(8,128)} %tile.5), calls=%async_computation.3 | async-start | bytes 524288 | tf_op jit(solution)/shard_map/all_to_all | solution.py:286
  188.7 1.3 convert_add_fusion
  190.0 2.3 %collective-permute-start.41 = (bf16[3,128,256]{2,1,0:T(8,128)(2,1)S(1)}, bf16[3,128,256]{2,1,0:T(8,128)(2,1)S(1)}, u32[]{:S(2)}, u32[]{:S(2)}) collective-permute-start(bf16[3,128,256]{2,1,0:T(8,128)(2,1)S(1)} %slice.183), channel_id=1, source_target_pairs={{0,128},{128,0},{1,129},{129,1},{2,130},{130,2},{3,131},{131,3},{4... | collective-permute-start | bytes 589832 | tf_op jit(solution)/shard_map/ppermute | solution.py:39
  192.3 0.6 slice.149
  192.8 2.2 %all-to-all-done.3 = f32[8,32,256]{2,1,0:T(8,128)S(1)} async-done(((f32[8,32,256]{2,1,0:T(8,128)}), f32[8,32,256]{2,1,0:T(8,128)S(1)}, u32[]{:S(2)}, u32[]{:S(2)}) %all-to-all-start.3) | async-done | bytes 262176 | tf_op jit(solution)/shard_map/all_to_all | solution.py:286
  195.0 2.3 %collective-permute-done.41 = bf16[3,128,256]{2,1,0:T(8,128)(2,1)S(1)} collective-permute-done((bf16[3,128,256]{2,1,0:T(8,128)(2,1)S(1)}, bf16[3,128,256]{2,1,0:T(8,128)(2,1)S(1)}, u32[]{:S(2)}, u32[]{:S(2)}) %collective-permute-start.41) | collective-permute-done | bytes 196640 | tf_op jit(solution)/shard_map/ppermute | solution.py:39
  197.3 0.7 fusion
  198.0 0.7 copy.12
  (132 shorter events, 2.3 us)
Async XLA Ops:
  0.6 10.4 %collective-permute-start.7 = (bf16[3,128,256]{2,1,0:T(8,128)(2,1)}, bf16[3,128,256]{2,1,0:T(8,128)(2,1)S(1)}, u32[]{:S(2)}, u32[]{:S(2)}) collective-permute-start(bf16[3,128,256]{2,1,0:T(8,128)(2,1)} %bitcast.18), channel_id=1, source_target_pairs={{0,112},{16,0},{32,16},{48,32},{64,48},{80,64},{96,80},{112,96},{1... | collective-permute-start | bytes 589832 | tf_op jit(solution)/shard_map/ppermute | solution.py:43
  6.6 8.1 %collective-permute-start.3 = (bf16[3,128,256]{2,1,0:T(8,128)(2,1)}, bf16[3,128,256]{2,1,0:T(8,128)(2,1)S(1)}, u32[]{:S(2)}, u32[]{:S(2)}) collective-permute-start(bf16[3,128,256]{2,1,0:T(8,128)(2,1)} %bitcast.19), channel_id=1, source_target_pairs={{0,16},{16,32},{32,48},{48,64},{64,80},{80,96},{96,112},{112,0},{1... | collective-permute-start | bytes 589832 | tf_op jit(solution)/shard_map/ppermute | solution.py:43
  6.6 8.2 %collective-permute-start.1 = (bf16[3,128,256]{2,1,0:T(8,128)(2,1)}, bf16[3,128,256]{2,1,0:T(8,128)(2,1)S(1)}, u32[]{:S(2)}, u32[]{:S(2)}) collective-permute-start(bf16[3,128,256]{2,1,0:T(8,128)(2,1)} %bitcast.20), channel_id=1, source_target_pairs={{0,8},{8,0},{1,9},{9,1},{2,10},{10,2},{3,11},{11,3},{4,12},{12,4},... | collective-permute-start | bytes 589832 | tf_op jit(solution)/shard_map/ppermute | solution.py:39
  6.6 9.0 %collective-permute-start = (bf16[3,128,256]{2,1,0:T(8,128)(2,1)}, bf16[3,128,256]{2,1,0:T(8,128)(2,1)S(1)}, u32[]{:S(2)}, u32[]{:S(2)}) collective-permute-start(bf16[3,128,256]{2,1,0:T(8,128)(2,1)} %bitcast.21), channel_id=1, source_target_pairs={{0,128},{128,0},{1,129},{129,1},{2,130},{130,2},{3,131},{131,3},{4... | collective-permute-start | bytes 589832 | tf_op jit(solution)/shard_map/ppermute | solution.py:39
  11.0 40.7 %copy-start.3 = (bf16[3,128,256]{2,1,0:T(8,128)(2,1)}, bf16[3,128,256]{2,1,0:T(8,128)(2,1)S(1)}, u32[]{:S(2)}) copy-start(bf16[3,128,256]{2,1,0:T(8,128)(2,1)S(1)} %collective-permute-done.7.refs_8_) | copy-start | bytes 589828
  11.0 7.8 %collective-permute-start.15 = (bf16[3,128,256]{2,1,0:T(8,128)(2,1)S(1)}, bf16[3,128,256]{2,1,0:T(8,128)(2,1)S(1)}, u32[]{:S(2)}, u32[]{:S(2)}) collective-permute-start(bf16[3,128,256]{2,1,0:T(8,128)(2,1)S(1)} %collective-permute-done.7.refs_8_), channel_id=1, source_target_pairs={{0,112},{16,0},{32,16},{48,32},{64,48},{80,64},{96,80},{112,96},{1... | collective-permute-start | bytes 589832 | tf_op jit(solution)/shard_map/ppermute | solution.py:43
  14.6 4.2 %collective-permute-start.9 = (bf16[3,128,256]{2,1,0:T(8,128)(2,1)S(1)}, bf16[3,128,256]{2,1,0:T(8,128)(2,1)S(1)}, u32[]{:S(2)}, u32[]{:S(2)}) collective-permute-start(bf16[3,128,256]{2,1,0:T(8,128)(2,1)S(1)} %collective-permute-done.7.refs_8_), channel_id=1, source_target_pairs={{0,8},{8,0},{1,9},{9,1},{2,10},{10,2},{3,11},{11,3},{4,12},{12,4},... | collective-permute-start | bytes 589832 | tf_op jit(solution)/shard_map/ppermute | solution.py:39
  14.6 37.1 %copy-start.4 = (bf16[3,128,256]{2,1,0:T(8,128)(2,1)}, bf16[3,128,256]{2,1,0:T(8,128)(2,1)S(1)}, u32[]{:S(2)}) copy-start(bf16[3,128,256]{2,1,0:T(8,128)(2,1)S(1)} %collective-permute-done.3.refs_4_) | copy-start | bytes 589828
  14.6 9.0 %collective-permute-start.11 = (bf16[3,128,256]{2,1,0:T(8,128)(2,1)S(1)}, bf16[3,128,256]{2,1,0:T(8,128)(2,1)S(1)}, u32[]{:S(2)}, u32[]{:S(2)}) collective-permute-start(bf16[3,128,256]{2,1,0:T(8,128)(2,1)S(1)} %collective-permute-done.3.refs_4_), channel_id=1, source_target_pairs={{0,16},{16,32},{32,48},{48,64},{64,80},{80,96},{96,112},{112,0},{1... | collective-permute-start | bytes 589832 | tf_op jit(solution)/shard_map/ppermute | solution.py:43
  14.7 37.0 %copy-start.5 = (bf16[3,128,256]{2,1,0:T(8,128)(2,1)}, bf16[3,128,256]{2,1,0:T(8,128)(2,1)S(1)}, u32[]{:S(2)}) copy-start(bf16[3,128,256]{2,1,0:T(8,128)(2,1)S(1)} %collective-permute-done.1.refs_2_) | copy-start | bytes 589828
  14.8 8.9 %collective-permute-start.5 = (bf16[3,128,256]{2,1,0:T(8,128)(2,1)S(1)}, bf16[3,128,256]{2,1,0:T(8,128)(2,1)S(1)}, u32[]{:S(2)}, u32[]{:S(2)}) collective-permute-start(bf16[3,128,256]{2,1,0:T(8,128)(2,1)S(1)} %collective-permute-done.3.refs_4_), channel_id=1, source_target_pairs={{0,8},{8,0},{1,9},{9,1},{2,10},{10,2},{3,11},{11,3},{4,12},{12,4},... | collective-permute-start | bytes 589832 | tf_op jit(solution)/shard_map/ppermute | solution.py:39
  15.6 36.2 %copy-start.6 = (bf16[3,128,256]{2,1,0:T(8,128)(2,1)}, bf16[3,128,256]{2,1,0:T(8,128)(2,1)S(1)}, u32[]{:S(2)}) copy-start(bf16[3,128,256]{2,1,0:T(8,128)(2,1)S(1)} %collective-permute-done.refs_1_) | copy-start | bytes 589828
  15.6 8.2 %collective-permute-start.8 = (bf16[3,128,256]{2,1,0:T(8,128)(2,1)S(1)}, bf16[3,128,256]{2,1,0:T(8,128)(2,1)S(1)}, u32[]{:S(2)}, u32[]{:S(2)}) collective-permute-start(bf16[3,128,256]{2,1,0:T(8,128)(2,1)S(1)} %collective-permute-done.refs_1_), channel_id=1, source_target_pairs={{0,112},{16,0},{32,16},{48,32},{64,48},{80,64},{96,80},{112,96},{1... | collective-permute-start | bytes 589832 | tf_op jit(solution)/shard_map/ppermute | solution.py:43
  18.8 33.0 %copy-start.7 = (bf16[3,128,256]{2,1,0:T(8,128)(2,1)}, bf16[3,128,256]{2,1,0:T(8,128)(2,1)S(1)}, u32[]{:S(2)}) copy-start(bf16[3,128,256]{2,1,0:T(8,128)(2,1)S(1)} %collective-permute-done.15.refs_16_) | copy-start | bytes 589828
  18.8 8.5 %collective-permute-start.4 = (bf16[3,128,256]{2,1,0:T(8,128)(2,1)S(1)}, bf16[3,128,256]{2,1,0:T(8,128)(2,1)S(1)}, u32[]{:S(2)}, u32[]{:S(2)}) collective-permute-start(bf16[3,128,256]{2,1,0:T(8,128)(2,1)S(1)} %collective-permute-done.refs_1_), channel_id=1, source_target_pairs={{0,16},{16,32},{32,48},{48,64},{64,80},{80,96},{96,112},{112,0},{1... | collective-permute-start | bytes 589832 | tf_op jit(solution)/shard_map/ppermute | solution.py:43
  18.9 32.9 %copy-start.8 = (bf16[3,128,256]{2,1,0:T(8,128)(2,1)}, bf16[3,128,256]{2,1,0:T(8,128)(2,1)S(1)}, u32[]{:S(2)}) copy-start(bf16[3,128,256]{2,1,0:T(8,128)(2,1)S(1)} %collective-permute-done.9.refs_10_) | copy-start | bytes 589828
  18.9 8.5 %collective-permute-start.2 = (bf16[3,128,256]{2,1,0:T(8,128)(2,1)S(1)}, bf16[3,128,256]{2,1,0:T(8,128)(2,1)S(1)}, u32[]{:S(2)}, u32[]{:S(2)}) collective-permute-start(bf16[3,128,256]{2,1,0:T(8,128)(2,1)S(1)} %collective-permute-done.refs_1_), channel_id=1, source_target_pairs={{0,8},{8,0},{1,9},{9,1},{2,10},{10,2},{3,11},{11,3},{4,12},{12,4},... | collective-permute-start | bytes 589832 | tf_op jit(solution)/shard_map/ppermute | solution.py:39
  23.6 28.2 %copy-start.9 = (bf16[3,128,256]{2,1,0:T(8,128)(2,1)}, bf16[3,128,256]{2,1,0:T(8,128)(2,1)S(1)}, u32[]{:S(2)}) copy-start(bf16[3,128,256]{2,1,0:T(8,128)(2,1)S(1)} %collective-permute-done.11.refs_12_) | copy-start | bytes 589828
  23.6 6.0 %collective-permute-start.23 = (bf16[3,128,256]{2,1,0:T(8,128)(2,1)S(1)}, bf16[3,128,256]{2,1,0:T(8,128)(2,1)S(1)}, u32[]{:S(2)}, u32[]{:S(2)}) collective-permute-start(bf16[3,128,256]{2,1,0:T(8,128)(2,1)S(1)} %collective-permute-done.15.refs_16_), channel_id=1, source_target_pairs={{0,112},{16,0},{32,16},{48,32},{64,48},{80,64},{96,80},{112,96},{1... | collective-permute-start | bytes 589832 | tf_op jit(solution)/shard_map/ppermute | solution.py:43
  23.6 28.2 %copy-start.10 = (bf16[3,128,256]{2,1,0:T(8,128)(2,1)}, bf16[3,128,256]{2,1,0:T(8,128)(2,1)S(1)}, u32[]{:S(2)}) copy-start(bf16[3,128,256]{2,1,0:T(8,128)(2,1)S(1)} %collective-permute-done.5.refs_6_) | copy-start | bytes 589828
  23.7 6.0 %collective-permute-start.17 = (bf16[3,128,256]{2,1,0:T(8,128)(2,1)S(1)}, bf16[3,128,256]{2,1,0:T(8,128)(2,1)S(1)}, u32[]{:S(2)}, u32[]{:S(2)}) collective-permute-start(bf16[3,128,256]{2,1,0:T(8,128)(2,1)S(1)} %collective-permute-done.15.refs_16_), channel_id=1, source_target_pairs={{0,8},{8,0},{1,9},{9,1},{2,10},{10,2},{3,11},{11,3},{4,12},{12,4},... | collective-permute-start | bytes 589832 | tf_op jit(solution)/shard_map/ppermute | solution.py:39
  23.8 28.1 %copy-start.11 = (bf16[3,128,256]{2,1,0:T(8,128)(2,1)}, bf16[3,128,256]{2,1,0:T(8,128)(2,1)S(1)}, u32[]{:S(2)}) copy-start(bf16[3,128,256]{2,1,0:T(8,128)(2,1)S(1)} %collective-permute-done.8.refs_9_) | copy-start | bytes 589828
  23.8 8.5 %collective-permute-start.19 = (bf16[3,128,256]{2,1,0:T(8,128)(2,1)S(1)}, bf16[3,128,256]{2,1,0:T(8,128)(2,1)S(1)}, u32[]{:S(2)}, u32[]{:S(2)}) collective-permute-start(bf16[3,128,256]{2,1,0:T(8,128)(2,1)S(1)} %collective-permute-done.11.refs_12_), channel_id=1, source_target_pairs={{0,16},{16,32},{32,48},{48,64},{64,80},{80,96},{96,112},{112,0},{1... | collective-permute-start | bytes 589832 | tf_op jit(solution)/shard_map/ppermute | solution.py:43
  27.4 24.4 %copy-start.12 = (bf16[3,128,256]{2,1,0:T(8,128)(2,1)}, bf16[3,128,256]{2,1,0:T(8,128)(2,1)S(1)}, u32[]{:S(2)}) copy-start(bf16[3,128,256]{2,1,0:T(8,128)(2,1)S(1)} %collective-permute-done.4.refs_5_) | copy-start | bytes 589828
  27.4 4.9 %collective-permute-start.13 = (bf16[3,128,256]{2,1,0:T(8,128)(2,1)S(1)}, bf16[3,128,256]{2,1,0:T(8,128)(2,1)S(1)}, u32[]{:S(2)}, u32[]{:S(2)}) collective-permute-start(bf16[3,128,256]{2,1,0:T(8,128)(2,1)S(1)} %collective-permute-done.11.refs_12_), channel_id=1, source_target_pairs={{0,8},{8,0},{1,9},{9,1},{2,10},{10,2},{3,11},{11,3},{4,12},{12,4},... | collective-permute-start | bytes 589832 | tf_op jit(solution)/shard_map/ppermute | solution.py:39
  27.4 24.4 %copy-start.13 = (bf16[3,128,256]{2,1,0:T(8,128)(2,1)}, bf16[3,128,256]{2,1,0:T(8,128)(2,1)S(1)}, u32[]{:S(2)}) copy-start(bf16[3,128,256]{2,1,0:T(8,128)(2,1)S(1)} %collective-permute-done.2.refs_3_) | copy-start | bytes 589828
  27.4 7.3 %collective-permute-start.16 = (bf16[3,128,256]{2,1,0:T(8,128)(2,1)S(1)}, bf16[3,128,256]{2,1,0:T(8,128)(2,1)S(1)}, u32[]{:S(2)}, u32[]{:S(2)}) collective-permute-start(bf16[3,128,256]{2,1,0:T(8,128)(2,1)S(1)} %collective-permute-done.8.refs_9_), channel_id=1, source_target_pairs={{0,112},{16,0},{32,16},{48,32},{64,48},{80,64},{96,80},{112,96},{1... | collective-permute-start | bytes 589832 | tf_op jit(solution)/shard_map/ppermute | solution.py:43
  29.6 22.2 %copy-start.14 = (bf16[3,128,256]{2,1,0:T(8,128)(2,1)}, bf16[3,128,256]{2,1,0:T(8,128)(2,1)S(1)}, u32[]{:S(2)}) copy-start(bf16[3,128,256]{2,1,0:T(8,128)(2,1)S(1)} %collective-permute-done.23.refs_24_) | copy-start | bytes 589828
  29.6 8.6 %collective-permute-start.10 = (bf16[3,128,256]{2,1,0:T(8,128)(2,1)S(1)}, bf16[3,128,256]{2,1,0:T(8,128)(2,1)S(1)}, u32[]{:S(2)}, u32[]{:S(2)}) collective-permute-start(bf16[3,128,256]{2,1,0:T(8,128)(2,1)S(1)} %collective-permute-done.8.refs_9_), channel_id=1, source_target_pairs={{0,8},{8,0},{1,9},{9,1},{2,10},{10,2},{3,11},{11,3},{4,12},{12,4},... | collective-permute-start | bytes 589832 | tf_op jit(solution)/shard_map/ppermute | solution.py:39
  29.6 22.2 %copy-start.15 = (bf16[3,128,256]{2,1,0:T(8,128)(2,1)}, bf16[3,128,256]{2,1,0:T(8,128)(2,1)S(1)}, u32[]{:S(2)}) copy-start(bf16[3,128,256]{2,1,0:T(8,128)(2,1)S(1)} %collective-permute-done.17.refs_18_) | copy-start | bytes 589828
  29.7 9.1 %collective-permute-start.12 = (bf16[3,128,256]{2,1,0:T(8,128)(2,1)S(1)}, bf16[3,128,256]{2,1,0:T(8,128)(2,1)S(1)}, u32[]{:S(2)}, u32[]{:S(2)}) collective-permute-start(bf16[3,128,256]{2,1,0:T(8,128)(2,1)S(1)} %collective-permute-done.4.refs_5_), channel_id=1, source_target_pairs={{0,16},{16,32},{32,48},{48,64},{64,80},{80,96},{96,112},{112,0},{1... | collective-permute-start | bytes 589832 | tf_op jit(solution)/shard_map/ppermute | solution.py:43
  32.3 19.6 %copy-start.16 = (bf16[3,128,256]{2,1,0:T(8,128)(2,1)}, bf16[3,128,256]{2,1,0:T(8,128)(2,1)S(1)}, u32[]{:S(2)}) copy-start(bf16[3,128,256]{2,1,0:T(8,128)(2,1)S(1)} %collective-permute-done.19.refs_20_) | copy-start | bytes 589828
  32.3 6.5 %collective-permute-start.6 = (bf16[3,128,256]{2,1,0:T(8,128)(2,1)S(1)}, bf16[3,128,256]{2,1,0:T(8,128)(2,1)S(1)}, u32[]{:S(2)}, u32[]{:S(2)}) collective-permute-start(bf16[3,128,256]{2,1,0:T(8,128)(2,1)S(1)} %collective-permute-done.4.refs_5_), channel_id=1, source_target_pairs={{0,8},{8,0},{1,9},{9,1},{2,10},{10,2},{3,11},{11,3},{4,12},{12,4},... | collective-permute-start | bytes 589832 | tf_op jit(solution)/shard_map/ppermute | solution.py:39
  32.3 19.6 %copy-start.17 = (bf16[3,128,256]{2,1,0:T(8,128)(2,1)}, bf16[3,128,256]{2,1,0:T(8,128)(2,1)S(1)}, u32[]{:S(2)}) copy-start(bf16[3,128,256]{2,1,0:T(8,128)(2,1)S(1)} %collective-permute-done.13.refs_14_) | copy-start | bytes 589828
  32.3 7.0 %collective-permute-start.25 = (bf16[3,128,256]{2,1,0:T(8,128)(2,1)S(1)}, bf16[3,128,256]{2,1,0:T(8,128)(2,1)S(1)}, u32[]{:S(2)}, u32[]{:S(2)}) collective-permute-start(bf16[3,128,256]{2,1,0:T(8,128)(2,1)S(1)} %collective-permute-done.23.refs_24_), channel_id=1, source_target_pairs={{0,8},{8,0},{1,9},{9,1},{2,10},{10,2},{3,11},{11,3},{4,12},{12,4},... | collective-permute-start | bytes 589832 | tf_op jit(solution)/shard_map/ppermute | solution.py:39
  34.7 17.2 %copy-start.18 = (bf16[3,128,256]{2,1,0:T(8,128)(2,1)}, bf16[3,128,256]{2,1,0:T(8,128)(2,1)S(1)}, u32[]{:S(2)}) copy-start(bf16[3,128,256]{2,1,0:T(8,128)(2,1)S(1)} %collective-permute-done.16.refs_17_) | copy-start | bytes 589828
  34.7 6.4 %collective-permute-start.24 = (bf16[3,128,256]{2,1,0:T(8,128)(2,1)S(1)}, bf16[3,128,256]{2,1,0:T(8,128)(2,1)S(1)}, u32[]{:S(2)}, u32[]{:S(2)}) collective-permute-start(bf16[3,128,256]{2,1,0:T(8,128)(2,1)S(1)} %collective-permute-done.16.refs_17_), channel_id=1, source_target_pairs={{0,112},{16,0},{32,16},{48,32},{64,48},{80,64},{96,80},{112,96},{1... | collective-permute-start | bytes 589832 | tf_op jit(solution)/shard_map/ppermute | solution.py:43
  38.3 9.0 %collective-permute-start.27 = (bf16[3,128,256]{2,1,0:T(8,128)(2,1)S(1)}, bf16[3,128,256]{2,1,0:T(8,128)(2,1)S(1)}, u32[]{:S(2)}, u32[]{:S(2)}) collective-permute-start(bf16[3,128,256]{2,1,0:T(8,128)(2,1)S(1)} %collective-permute-done.19.refs_20_), channel_id=1, source_target_pairs={{0,16},{16,32},{32,48},{48,64},{64,80},{80,96},{96,112},{112,0},{1... | collective-permute-start | bytes 589832 | tf_op jit(solution)/shard_map/ppermute | solution.py:43
  38.8 8.5 %collective-permute-start.21 = (bf16[3,128,256]{2,1,0:T(8,128)(2,1)S(1)}, bf16[3,128,256]{2,1,0:T(8,128)(2,1)S(1)}, u32[]{:S(2)}, u32[]{:S(2)}) collective-permute-start(bf16[3,128,256]{2,1,0:T(8,128)(2,1)S(1)} %collective-permute-done.19.refs_20_), channel_id=1, source_target_pairs={{0,8},{8,0},{1,9},{9,1},{2,10},{10,2},{3,11},{11,3},{4,12},{12,4},... | collective-permute-start | bytes 589832 | tf_op jit(solution)/shard_map/ppermute | solution.py:39
  38.8 9.0 %collective-permute-start.18 = (bf16[3,128,256]{2,1,0:T(8,128)(2,1)S(1)}, bf16[3,128,256]{2,1,0:T(8,128)(2,1)S(1)}, u32[]{:S(2)}, u32[]{:S(2)}) collective-permute-start(bf16[3,128,256]{2,1,0:T(8,128)(2,1)S(1)} %collective-permute-done.16.refs_17_), channel_id=1, source_target_pairs={{0,8},{8,0},{1,9},{9,1},{2,10},{10,2},{3,11},{11,3},{4,12},{12,4},... | collective-permute-start | bytes 589832 | tf_op jit(solution)/shard_map/ppermute | solution.py:39
  39.3 10.7 %collective-permute-start.20 = (bf16[3,128,256]{2,1,0:T(8,128)(2,1)S(1)}, bf16[3,128,256]{2,1,0:T(8,128)(2,1)S(1)}, u32[]{:S(2)}, u32[]{:S(2)}) collective-permute-start(bf16[3,128,256]{2,1,0:T(8,128)(2,1)S(1)} %collective-permute-done.12.refs_13_), channel_id=1, source_target_pairs={{0,16},{16,32},{32,48},{48,64},{64,80},{80,96},{96,112},{112,0},{1... | collective-permute-start | bytes 589832 | tf_op jit(solution)/shard_map/ppermute | solution.py:43
  41.2 8.9 %collective-permute-start.28 = (bf16[3,128,256]{2,1,0:T(8,128)(2,1)S(1)}, bf16[3,128,256]{2,1,0:T(8,128)(2,1)S(1)}, u32[]{:S(2)}, u32[]{:S(2)}) collective-permute-start(bf16[3,128,256]{2,1,0:T(8,128)(2,1)S(1)} %collective-permute-done.24.refs_25_), channel_id=1, source_target_pairs={{0,112},{16,0},{32,16},{48,32},{64,48},{80,64},{96,80},{112,96},{1... | collective-permute-start | bytes 589832 | tf_op jit(solution)/shard_map/ppermute | solution.py:43
  47.3 3.9 %collective-permute-start.14 = (bf16[3,128,256]{2,1,0:T(8,128)(2,1)S(1)}, bf16[3,128,256]{2,1,0:T(8,128)(2,1)S(1)}, u32[]{:S(2)}, u32[]{:S(2)}) collective-permute-start(bf16[3,128,256]{2,1,0:T(8,128)(2,1)S(1)} %collective-permute-done.12.refs_13_), channel_id=1, source_target_pairs={{0,8},{8,0},{1,9},{9,1},{2,10},{10,2},{3,11},{11,3},{4,12},{12,4},... | collective-permute-start | bytes 589832 | tf_op jit(solution)/shard_map/ppermute | solution.py:39
  47.3 3.9 %collective-permute-start.26 = (bf16[3,128,256]{2,1,0:T(8,128)(2,1)S(1)}, bf16[3,128,256]{2,1,0:T(8,128)(2,1)S(1)}, u32[]{:S(2)}, u32[]{:S(2)}) collective-permute-start(bf16[3,128,256]{2,1,0:T(8,128)(2,1)S(1)} %collective-permute-done.24.refs_25_), channel_id=1, source_target_pairs={{0,8},{8,0},{1,9},{9,1},{2,10},{10,2},{3,11},{11,3},{4,12},{12,4},... | collective-permute-start | bytes 589832 | tf_op jit(solution)/shard_map/ppermute | solution.py:39
  47.8 3.3 %collective-permute-start.29 = (bf16[3,128,256]{2,1,0:T(8,128)(2,1)S(1)}, bf16[3,128,256]{2,1,0:T(8,128)(2,1)S(1)}, u32[]{:S(2)}, u32[]{:S(2)}) collective-permute-start(bf16[3,128,256]{2,1,0:T(8,128)(2,1)S(1)} %collective-permute-done.27.refs_28_), channel_id=1, source_target_pairs={{0,8},{8,0},{1,9},{9,1},{2,10},{10,2},{3,11},{11,3},{4,12},{12,4},... | collective-permute-start | bytes 589832 | tf_op jit(solution)/shard_map/ppermute | solution.py:39
  50.0 1.4 collective-permute-start.22
  50.1 1.7 collective-permute-start.30
  131.6 3.7 %collective-permute-start.32 = (bf16[24,128,256]{2,1,0:T(8,128)(2,1)}, bf16[24,128,256]{2,1,0:T(8,128)(2,1)S(1)}, u32[]{:S(2)}, u32[]{:S(2)}) collective-permute-start(bf16[24,128,256]{2,1,0:T(8,128)(2,1)} %get-tuple-element.15), channel_id=1, source_target_pairs={{0,8},{8,0},{1,9},{9,1},{2,10},{10,2},{3,11},{11,3},{4,12},{12,4},... | collective-permute-start | bytes 4718600 | tf_op jit(solution)/shard_map/ppermute | solution.py:39
  131.7 6.4 %collective-permute-start.31 = (bf16[24,128,256]{2,1,0:T(8,128)(2,1)}, bf16[24,128,256]{2,1,0:T(8,128)(2,1)S(1)}, u32[]{:S(2)}, u32[]{:S(2)}) collective-permute-start(bf16[24,128,256]{2,1,0:T(8,128)(2,1)} %get-tuple-element.13), channel_id=1, source_target_pairs={{0,8},{8,0},{1,9},{9,1},{2,10},{10,2},{3,11},{11,3},{4,12},{12,4},... | collective-permute-start | bytes 4718600 | tf_op jit(solution)/shard_map/ppermute | solution.py:39
  133.1 13.5 %collective-permute-start.42 = (bf16[48,256]{1,0:T(8,128)(2,1)S(1)}, bf16[48,256]{1,0:T(8,128)(2,1)S(1)}, u32[]{:S(2)}, u32[]{:S(2)}) collective-permute-start(bf16[48,256]{1,0:T(8,128)(2,1)S(1)} %slice_reduce_fusion), channel_id=1, source_target_pairs={{0,8},{8,0},{1,9},{9,1},{2,10},{10,2},{3,11},{11,3},{4,12},{12,4},... | collective-permute-start | bytes 73736 | tf_op jit(solution)/shard_map/ppermute | solution.py:39
  135.3 19.5 %copy-start.2 = (bf16[24,128,256]{2,1,0:T(8,128)(2,1)}, bf16[24,128,256]{2,1,0:T(8,128)(2,1)S(1)}, u32[]{:S(2)}) copy-start(bf16[24,128,256]{2,1,0:T(8,128)(2,1)S(1)} %collective-permute-done.32) | copy-start | bytes 4718596
  137.3 7.0 %collective-permute-start.37 = (bf16[3,128,256]{2,1,0:T(8,128)(2,1)S(1)}, bf16[3,128,256]{2,1,0:T(8,128)(2,1)S(1)}, u32[]{:S(2)}, u32[]{:S(2)}) collective-permute-start(bf16[3,128,256]{2,1,0:T(8,128)(2,1)S(1)} %get-tuple-element.24), channel_id=1, source_target_pairs={{0,112},{16,0},{32,16},{48,32},{64,48},{80,64},{96,80},{112,96},{1... | collective-permute-start | bytes 589832 | tf_op jit(solution)/shard_map/ppermute | solution.py:43
  138.1 35.2 %copy-start.1 = (bf16[24,128,256]{2,1,0:T(8,128)(2,1)}, bf16[24,128,256]{2,1,0:T(8,128)(2,1)S(1)}, u32[]{:S(2)}) copy-start(bf16[24,128,256]{2,1,0:T(8,128)(2,1)S(1)} %collective-permute-done.31) | copy-start | bytes 4718596
  138.2 8.2 %collective-permute-start.33 = (bf16[3,128,256]{2,1,0:T(8,128)(2,1)S(1)}, bf16[3,128,256]{2,1,0:T(8,128)(2,1)S(1)}, u32[]{:S(2)}, u32[]{:S(2)}) collective-permute-start(bf16[3,128,256]{2,1,0:T(8,128)(2,1)S(1)} %get-tuple-element.23), channel_id=1, source_target_pairs={{0,16},{16,32},{32,48},{48,64},{64,80},{80,96},{96,112},{112,0},{1... | collective-permute-start | bytes 589832 | tf_op jit(solution)/shard_map/ppermute | solution.py:43
  144.4 10.4 %collective-permute-start.38 = (bf16[6,128,256]{2,1,0:T(8,128)(2,1)S(1)}, bf16[6,128,256]{2,1,0:T(8,128)(2,1)S(1)}, u32[]{:S(2)}, u32[]{:S(2)}) collective-permute-start(bf16[6,128,256]{2,1,0:T(8,128)(2,1)S(1)} %pad_maximum_fusion.1), channel_id=1, source_target_pairs={{0,112},{16,0},{32,16},{48,32},{64,48},{80,64},{96,80},{112,96},{1... | collective-permute-start | bytes 1179656 | tf_op jit(solution)/shard_map/ppermute | solution.py:43
  146.5 13.3 %collective-permute-start.34 = (bf16[6,128,256]{2,1,0:T(8,128)(2,1)S(1)}, bf16[6,128,256]{2,1,0:T(8,128)(2,1)S(1)}, u32[]{:S(2)}, u32[]{:S(2)}) collective-permute-start(bf16[6,128,256]{2,1,0:T(8,128)(2,1)S(1)} %pad_maximum_fusion), channel_id=1, source_target_pairs={{0,16},{16,32},{32,48},{48,64},{64,80},{80,96},{96,112},{112,0},{1... | collective-permute-start | bytes 1179656 | tf_op jit(solution)/shard_map/ppermute | solution.py:43
  146.7 14.1 %collective-permute-start.43 = (bf16[48,256]{1,0:T(8,128)(2,1)S(1)}, bf16[48,256]{1,0:T(8,128)(2,1)S(1)}, u32[]{:S(2)}, u32[]{:S(2)}) collective-permute-start(bf16[48,256]{1,0:T(8,128)(2,1)S(1)} %add_convert_fusion.5), channel_id=1, source_target_pairs={{0,128},{128,0},{1,129},{129,1},{2,130},{130,2},{3,131},{131,3},{4... | collective-permute-start | bytes 73736 | tf_op jit(solution)/shard_map/ppermute | solution.py:39
  156.7 11.2 %collective-permute-start.39 = (bf16[6,128,256]{2,1,0:T(8,128)(2,1)}, bf16[6,128,256]{2,1,0:T(8,128)(2,1)}, u32[]{:S(2)}, u32[]{:S(2)}) collective-permute-start(bf16[6,128,256]{2,1,0:T(8,128)(2,1)} %add_convert_fusion.1), channel_id=1, source_target_pairs={{0,112},{16,0},{32,16},{48,32},{64,48},{80,64},{96,80},{112,96},{1... | collective-permute-start | bytes 1179656 | tf_op jit(solution)/shard_map/ppermute | solution.py:43
  160.8 12.5 %collective-permute-start.35 = (bf16[6,128,256]{2,1,0:T(8,128)(2,1)}, bf16[6,128,256]{2,1,0:T(8,128)(2,1)}, u32[]{:S(2)}, u32[]{:S(2)}) collective-permute-start(bf16[6,128,256]{2,1,0:T(8,128)(2,1)} %add_convert_fusion.3), channel_id=1, source_target_pairs={{0,16},{16,32},{32,48},{48,64},{64,80},{80,96},{96,112},{112,0},{1... | collective-permute-start | bytes 1179656 | tf_op jit(solution)/shard_map/ppermute | solution.py:43
  161.5 15.5 %all-to-all-start.2 = ((bf16[8,48,256]{2,1,0:T(8,128)(2,1)}), bf16[8,48,256]{2,1,0:T(8,128)(2,1)S(1)}, u32[]{:S(2)}, u32[]{:S(2)}) async-start(bf16[8,48,256]{2,1,0:T(8,128)(2,1)} %tile.4), calls=%async_computation.2 | async-start | bytes 393216 | tf_op jit(solution)/shard_map/all_to_all | solution.py:283
  170.1 18.6 %collective-permute-start.40 = (bf16[6,128,256]{2,1,0:T(8,128)(2,1)}, bf16[6,128,256]{2,1,0:T(8,128)(2,1)}, u32[]{:S(2)}, u32[]{:S(2)}) collective-permute-start(bf16[6,128,256]{2,1,0:T(8,128)(2,1)} %add_convert_fusion), channel_id=1, source_target_pairs={{0,112},{16,0},{32,16},{48,32},{64,48},{80,64},{96,80},{112,96},{1... | collective-permute-start | bytes 1179656 | tf_op jit(solution)/shard_map/ppermute | solution.py:43
  175.2 13.5 %collective-permute-start.36 = (bf16[6,128,256]{2,1,0:T(8,128)(2,1)}, bf16[6,128,256]{2,1,0:T(8,128)(2,1)S(1)}, u32[]{:S(2)}, u32[]{:S(2)}) collective-permute-start(bf16[6,128,256]{2,1,0:T(8,128)(2,1)} %add_convert_fusion.2), channel_id=1, source_target_pairs={{0,16},{16,32},{32,48},{48,64},{64,80},{80,96},{96,112},{112,0},{1... | collective-permute-start | bytes 1179656 | tf_op jit(solution)/shard_map/ppermute | solution.py:43
  178.5 16.5 %all-to-all-start.3 = ((f32[8,32,256]{2,1,0:T(8,128)}), f32[8,32,256]{2,1,0:T(8,128)S(1)}, u32[]{:S(2)}, u32[]{:S(2)}) async-start(f32[8,32,256]{2,1,0:T(8,128)} %tile.5), calls=%async_computation.3 | async-start | bytes 524288 | tf_op jit(solution)/shard_map/all_to_all | solution.py:286
  190.0 7.3 %collective-permute-start.41 = (bf16[3,128,256]{2,1,0:T(8,128)(2,1)S(1)}, bf16[3,128,256]{2,1,0:T(8,128)(2,1)S(1)}, u32[]{:S(2)}, u32[]{:S(2)}) collective-permute-start(bf16[3,128,256]{2,1,0:T(8,128)(2,1)S(1)} %slice.183), channel_id=1, source_target_pairs={{0,128},{128,0},{1,129},{129,1},{2,130},{130,2},{3,131},{131,3},{4... | collective-permute-start | bytes 589832 | tf_op jit(solution)/shard_map/ppermute | solution.py:39
  (16 other events, 87.4 us)
where the time goes:
time: 200 us; the launch traced here: 199 us
  starting transfers between devices  61.8 us (31%)
  blocking collectives  54.8 us (27%)
  waiting for transfers between devices  35.9 us (18%)
  Pallas kernels  24.3 us (12%)
  other arithmetic  17.4 us (9%)
  local copies, waits for them, and re-layouts  3.32 us (2%)
    ppermute x22, starting transfers between devices, turn(): return lax.ppermute(v, 'z', [(i, (i + step) % Z) for i in range(Z)])  32 us
    all_to_all x1, blocking collectives, shards(): back = lax.all_to_all(back, BLK, split_axis=0, concat_axis=0, tiled=True)  28.9 us
    ppermute x22, waiting for transfers between devices, turn(): return lax.ppermute(v, 'z', [(i, (i + step) % Z) for i in range(Z)])  26.7 us
    all_to_all x1, blocking collectives, shards(): lax.all_to_all(partial.reshape(N_BLK, NB, HIDDEN), BLK, split_axis=0, con...  25.9 us
    ppermute x22, starting transfers between devices, swap(): return lambda v: lax.ppermute(v, axis, [(0, 1), (1, 0)])  13.2 us
    pallas_call x1, Pallas kernels, backward_tiles(): pl.pallas_call(backward_kernel, out_shape=[jax.ShapeDtypeStruct((CHAIN, T...  10.7 us
    pallas_call x1, Pallas kernels, forward_tiles(): pl.pallas_call(forward_kernel, out_shape=jax.ShapeDtypeStruct((TR, TILE,...  10.1 us
    all_to_all x1, starting transfers between devices, shards(): lax.all_to_all(jnp.tile(grads[:GRAD_ROWS], (N_BLK, 1)), BLK, split_axis=0...  10.1 us
  transfers between devices with their start and end apart: 46, of which 18 were waited for; matrix products, arithmetic and copies ran while one was open for 9% of the time, Pallas kernels for 0%

commit v1 on v0

--- a/solution.py
+++ b/solution.py
@@ -138,19 +138,22 @@
         return carry
 
     lax.fori_loop(0, groups, step, 0)
-    for i, out in enumerate(outs):
-        out[...] = acc[i * CHAIN : (i + 1) * CHAIN].astype(bf16)
+    at = 0
+    for out in outs:
+        out[...] = acc[at : at + out.shape[0]].astype(bf16)
+        at += out.shape[0]
 
 
 def backward_tiles(live, rows, pos, adj, err):
     return pl.pallas_call(
         backward_kernel,
-        out_shape=[jax.ShapeDtypeStruct((CHAIN, TILE, HIDDEN), bf16)] * (TC // CHAIN),
+        out_shape=[jax.ShapeDtypeStruct((XH * PER, TILE, HIDDEN), bf16)] * Z
+        + [jax.ShapeDtypeStruct((CHAIN, TILE, HIDDEN), bf16)] * 2,
         grid_spec=pltpu.PrefetchScalarGridSpec(
             num_scalar_prefetch=3,
             grid=(),
             in_specs=[ANY, ANY],
-            out_specs=[VMEM] * (TC // CHAIN),
+            out_specs=[VMEM] * (Z + 2),
             scratch_shapes=[
                 pltpu.VMEM((GROUPS, GROUP, TILE, TILE), bf16),
                 pltpu.VMEM((TR, TILE, HIDDEN), bf16),
@@ -232,7 +235,7 @@
 
     def mine(near):
         at = slice(near // 2 * XH * PER, (near // 2 + 1) * XH * PER)
-        return keep[near % 2][at].astype(f32) + received[near % 2][at].astype(f32)
+        return keep[near].astype(f32) + received[near % 2][at].astype(f32)
 
     far = mine(7).astype(bf16)
     right, left = turn(far[:PER], 1), turn(far[PER:], -1)
@@ -263,7 +266,8 @@
     live = jnp.sum((cols < TC).astype(jnp.int32)).reshape(1)
     near, other, across, part = place_of(jnp.minimum(cols, TC - 1), xh, z, core)
     slab_pos = ((near * CORE + other) * XH + across) * PER + part
-    sum_pos = (((other * 2 + near % 2) * (Z // 2) + near // 2) * XH + across) * PER + part
+    place = jnp.where(other == 0, near, Z + near % 2 * (Z // 2) + near // 2)
+    sum_pos = (place * XH + across) * PER + part
 
     pieces = gather_pieces(features.reshape(PER, TILE, HIDDEN))
     partial = forward_tiles(live, rows, slab_pos, adj, pieces)
@@ -275,7 +279,7 @@
     back = lax.all_to_all(back, BLK, split_axis=0, concat_axis=0, tiled=True)
 
     outs = backward_tiles(live, rows, sum_pos, adj, back)
-    grad_x, first, third = scatter_sum(outs[:2], outs[2:])
+    grad_x, first, third = scatter_sum(outs[:Z], outs[Z:])
 
     grads = jnp.sum(back[:, NB:].astype(f32), axis=0)
     grads = both_sides(both_sides(grads, "core"), "xh")

time: 200 us -> 200 us (level)
  waiting for transfers between devices: 35.9 us -> 45.6 us
  starting transfers between devices: 61.8 us -> 57.6 us
  other arithmetic: 17.4 us -> 13.6 us
  Pallas kernels: 24.3 us -> 20.6 us
    ppermute x22, waiting for transfers between devices: 26.7 us -> 36.8 us  [turn(): return lax.ppermute(v, 'z', [(i, (i + step) % Z) for i in range(Z)])]
    ppermute x22, starting transfers between devices: 32 us -> 36.7 us  [turn(): return lax.ppermute(v, 'z', [(i, (i + step) % Z) for i in range(Z)])]
    ppermute x22, starting transfers between devices: 13.2 us -> 9.56 us  [swap(): return lambda v: lax.ppermute(v, axis, [(0, 1), (1, 0)])]
    all_to_all x1, blocking collectives: 25.9 us -> 29.6 us  [shards(): lax.all_to_all(partial.reshape(N_BLK, NB, HIDDEN), BLK, split_axis=0, con...]
    all_to_all x1, starting transfers between devices: 6.43 us -> 3.39 us  [shards(): lax.all_to_all(jnp.tile(grads, (Z, 1)), 'z', split_axis=0, concat_axis=0,...]
    all_to_all x1, starting transfers between devices: 10.1 us -> 7.94 us  [shards(): lax.all_to_all(jnp.tile(grads[:GRAD_ROWS], (N_BLK, 1)), BLK, split_axis=0...]
  transfers between devices with their start and end apart: 46 -> 46, of which waited for: 18 -> 19; matrix products, arithmetic and copies ran while one was open for 9% -> 8% of each run, Pallas kernels for 0% -> 0%
where the time goes in v1:
time: 200 us; the launch traced here: 199 us
  starting transfers between devices  57.6 us (29%)
  blocking collectives  56.5 us (28%)
  waiting for transfers between devices  45.6 us (23%)
  Pallas kernels  20.6 us (10%)
  other arithmetic  13.6 us (7%)
  local copies, waits for them, and re-layouts  4.01 us (2%)
    ppermute x22, waiting for transfers between devices, turn(): return lax.ppermute(v, 'z', [(i, (i + step) % Z) for i in range(Z)])  36.8 us
    ppermute x22, starting transfers between devices, turn(): return lax.ppermute(v, 'z', [(i, (i + step) % Z) for i in range(Z)])  36.7 us
    all_to_all x1, blocking collectives, shards(): lax.all_to_all(partial.reshape(N_BLK, NB, HIDDEN), BLK, split_axis=0, con...  29.6 us
    all_to_all x1, blocking collectives, shards(): back = lax.all_to_all(back, BLK, split_axis=0, concat_axis=0, tiled=True)  27 us
    ppermute x22, starting transfers between devices, swap(): return lambda v: lax.ppermute(v, axis, [(0, 1), (1, 0)])  9.56 us
    pallas_call x1, Pallas kernels, backward_tiles(): pl.pallas_call(backward_kernel, out_shape=[jax.ShapeDtypeStruct((XH * PER...  8.75 us
    pallas_call x1, Pallas kernels, forward_tiles(): pl.pallas_call(forward_kernel, out_shape=jax.ShapeDtypeStruct((TR, TILE,...  8.41 us
    all_to_all x1, starting transfers between devices, shards(): lax.all_to_all(jnp.tile(grads[:GRAD_ROWS], (N_BLK, 1)), BLK, split_axis=0...  7.94 us
  transfers between devices with their start and end apart: 46, of which 19 were waited for; matrix products, arithmetic and copies ran while one was open for 8% of the time, Pallas kernels for 0%

profile of v1, /device:TPU:2, one launch (start us, length us, event | category | flops | bytes accessed | tf_op | source)
XLA Modules:
  0.0 199.2 jit_solution(14939811125241189078)
XLA Ops:
  0.6 2.2 %collective-permute-start = (bf16[3,128,256]{2,1,0:T(8,128)(2,1)}, bf16[3,128,256]{2,1,0:T(8,128)(2,1)S(1)}, u32[]{:S(2)}, u32[]{:S(2)}) collective-permute-start(bf16[3,128,256]{2,1,0:T(8,128)(2,1)} %bitcast.18), channel_id=1, source_target_pairs={{0,128},{128,0},{1,129},{129,1},{2,130},{130,2},{3,131},{131,3},{4... | collective-permute-start | bytes 589832 | tf_op jit(solution)/shard_map/ppermute | solution.py:39
  2.8 1.9 collective-permute-start.3
  4.8 3.9 %collective-permute-start.7 = (bf16[3,128,256]{2,1,0:T(8,128)(2,1)}, bf16[3,128,256]{2,1,0:T(8,128)(2,1)S(1)}, u32[]{:S(2)}, u32[]{:S(2)}) collective-permute-start(bf16[3,128,256]{2,1,0:T(8,128)(2,1)} %bitcast.20), channel_id=1, source_target_pairs={{0,112},{16,0},{32,16},{48,32},{64,48},{80,64},{96,80},{112,96},{1... | collective-permute-start | bytes 589832 | tf_op jit(solution)/shard_map/ppermute | solution.py:43
  8.7 0.4 collective-permute-done.refs_1_
  9.1 5.9 %collective-permute-start.8 = (bf16[3,128,256]{2,1,0:T(8,128)(2,1)S(1)}, bf16[3,128,256]{2,1,0:T(8,128)(2,1)S(1)}, u32[]{:S(2)}, u32[]{:S(2)}) collective-permute-start(bf16[3,128,256]{2,1,0:T(8,128)(2,1)S(1)} %collective-permute-done.refs_1_), channel_id=1, source_target_pairs={{0,112},{16,0},{32,16},{48,32},{64,48},{80,64},{96,80},{112,96},{1... | collective-permute-start | bytes 589832 | tf_op jit(solution)/shard_map/ppermute | solution.py:43
  15.1 3.2 %collective-permute-start.15 = (bf16[3,128,256]{2,1,0:T(8,128)(2,1)S(1)}, bf16[3,128,256]{2,1,0:T(8,128)(2,1)S(1)}, u32[]{:S(2)}, u32[]{:S(2)}) collective-permute-start(bf16[3,128,256]{2,1,0:T(8,128)(2,1)S(1)} %collective-permute-done.7.refs_8_), channel_id=1, source_target_pairs={{0,112},{16,0},{32,16},{48,32},{64,48},{80,64},{96,80},{112,96},{1... | collective-permute-start | bytes 589832 | tf_op jit(solution)/shard_map/ppermute | solution.py:43
  18.3 1.4 collective-permute-done.8.refs_9_
  19.7 4.1 %collective-permute-done.4.refs_5_ = bf16[3,128,256]{2,1,0:T(8,128)(2,1)S(1)} collective-permute-done((bf16[3,128,256]{2,1,0:T(8,128)(2,1)S(1)}, bf16[3,128,256]{2,1,0:T(8,128)(2,1)S(1)}, u32[]{:S(2)}, u32[]{:S(2)}) %collective-permute-start.4) | collective-permute-done | bytes 196640 | tf_op jit(solution)/shard_map/ppermute | solution.py:43
  23.7 2.1 %collective-permute-done.11.refs_12_ = bf16[3,128,256]{2,1,0:T(8,128)(2,1)S(1)} collective-permute-done((bf16[3,128,256]{2,1,0:T(8,128)(2,1)S(1)}, bf16[3,128,256]{2,1,0:T(8,128)(2,1)S(1)}, u32[]{:S(2)}, u32[]{:S(2)}) %collective-permute-start.11) | collective-permute-done | bytes 196640 | tf_op jit(solution)/shard_map/ppermute | solution.py:43
  25.9 2.0 %collective-permute-start.12 = (bf16[3,128,256]{2,1,0:T(8,128)(2,1)S(1)}, bf16[3,128,256]{2,1,0:T(8,128)(2,1)S(1)}, u32[]{:S(2)}, u32[]{:S(2)}) collective-permute-start(bf16[3,128,256]{2,1,0:T(8,128)(2,1)S(1)} %collective-permute-done.4.refs_5_), channel_id=1, source_target_pairs={{0,16},{16,32},{32,48},{48,64},{64,80},{80,96},{96,112},{112,0},{1... | collective-permute-start | bytes 589832 | tf_op jit(solution)/shard_map/ppermute | solution.py:43
  28.0 3.1 %collective-permute-start.23 = (bf16[3,128,256]{2,1,0:T(8,128)(2,1)S(1)}, bf16[3,128,256]{2,1,0:T(8,128)(2,1)S(1)}, u32[]{:S(2)}, u32[]{:S(2)}) collective-permute-start(bf16[3,128,256]{2,1,0:T(8,128)(2,1)S(1)} %collective-permute-done.15.refs_16_), channel_id=1, source_target_pairs={{0,112},{16,0},{32,16},{48,32},{64,48},{80,64},{96,80},{112,96},{1... | collective-permute-start | bytes 589832 | tf_op jit(solution)/shard_map/ppermute | solution.py:43
  31.1 1.3 reduce.2.row_ref
  32.4 0.8 collective-permute-done.16.refs_17_
  33.2 1.3 collective-permute-done.12.refs_13_
  34.5 2.1 %collective-permute-done.19.refs_20_ = bf16[3,128,256]{2,1,0:T(8,128)(2,1)S(1)} collective-permute-done((bf16[3,128,256]{2,1,0:T(8,128)(2,1)S(1)}, bf16[3,128,256]{2,1,0:T(8,128)(2,1)S(1)}, u32[]{:S(2)}, u32[]{:S(2)}) %collective-permute-start.19) | collective-permute-done | bytes 196640 | tf_op jit(solution)/shard_map/ppermute | solution.py:43
  36.6 1.4 collective-permute-start.24
  38.0 0.7 collective-permute-start.20
  38.7 0.7 compare_reduce_fusion
  39.4 1.3 remainder_reduce_fusion
  40.8 0.5 collective-permute-start.18
  41.3 0.4 collective-permute-start.27
  41.7 2.2 %collective-permute-done.24.refs_25_ = bf16[3,128,256]{2,1,0:T(8,128)(2,1)S(1)} collective-permute-done((bf16[3,128,256]{2,1,0:T(8,128)(2,1)S(1)}, bf16[3,128,256]{2,1,0:T(8,128)(2,1)S(1)}, u32[]{:S(2)}, u32[]{:S(2)}) %collective-permute-start.24) | collective-permute-done | bytes 196640 | tf_op jit(solution)/shard_map/ppermute | solution.py:43
  43.9 1.3 collective-permute-done.20.refs_21_
  45.2 0.3 collective-permute-start.28
  45.5 0.6 fusion.17
  46.1 3.3 %collective-permute-done.27.refs_28_ = bf16[3,128,256]{2,1,0:T(8,128)(2,1)S(1)} collective-permute-done((bf16[3,128,256]{2,1,0:T(8,128)(2,1)S(1)}, bf16[3,128,256]{2,1,0:T(8,128)(2,1)S(1)}, u32[]{:S(2)}, u32[]{:S(2)}) %collective-permute-start.27) | collective-permute-done | bytes 196640 | tf_op jit(solution)/shard_map/ppermute | solution.py:43
  49.5 0.5 collective-permute-start.26
  50.1 0.4 collective-permute-start.29
  50.5 0.8 collective-permute-done.28.refs_29_
  51.3 0.6 multiply_add_fusion.pos_ref
  52.0 0.7 collective-permute-done.30.refs_31_
  53.0 0.4 copy-done.36
  53.4 8.4 %forward_tiles.1 = bf16[24,128,256]{2,1,0:T(8,128)(2,1)} custom-call(s32[1]{0:T(128)} %bitcast.live_ref, s32[288]{0:T(512)} %reduce.2.row_ref, s32[288]{0:T(512)} %multiply_add_fusion.pos_ref, bf16[288,128,128]{2,1,0:T(8,128)(2,1)} %bitcast.14, bf16[3,128,256]{2,1,0:T(8,128)(2,1)} %bitcast.22, bf16[3,128,256]{2,1,0:T(8,128)(2,1)} %copy-done.6, ...), custom_call_target="tpu_custom_call" | custom-call | flops 2415919104 | bytes 28311552 | tf_op jit(solution)/shard_map/forward_tiles/pallas_call | solution.py:92
  61.8 29.6 %all_to_all.25.parts_ref = bf16[8,384,256]{2,1,0:T(8,128)(2,1)} all-to-all(bf16[8,384,256]{2,1,0:T(8,128)(2,1)} %bitcast.16), channel_id=1, replica_groups=mesh['xh'=2,'z'=8,'core'=2,'y'=4,'xl'=2] {'y','xl'}, dimensions={0} | all-to-all | bytes 3145728 | tf_op jit(solution)/shard_map/all_to_all | solution.py:274
  91.3 3.5 %dense_block.1 = (bf16[384,256]{1,0:T(8,128)(2,1)}, bf16[8,432,256]{2,1,0:T(8,128)(2,1)}) custom-call(bf16[8,384,256]{2,1,0:T(8,128)(2,1)} %all_to_all.25.parts_ref, bf16[256,256]{1,0:T(8,128)(2,1)} %weight_ref.1, f32[1,256]{1,0:T(1,128)} %bitcast.24, bf16[384,256]{1,0:T(8,128)(2,1)} %cot_ref.1), custom_call_target="tpu_custom_call" | custom-call | tf_op jit(solution)/shard_map/dense_block/pallas_call | solution.py:197
  94.8 27.0 %all_to_all.26.err_hbm = bf16[8,432,256]{2,1,0:T(8,128)(2,1)} all-to-all(bf16[8,432,256]{2,1,0:T(8,128)(2,1)} %get-tuple-element.17), channel_id=1, replica_groups=mesh['xh'=2,'z'=8,'core'=2,'y'=4,'xl'=2] {'y','xl'}, dimensions={0} | all-to-all | bytes 3538944 | tf_op jit(solution)/shard_map/all_to_all | solution.py:279
  121.8 8.7 %backward_tiles.1 = (bf16[6,128,256]{2,1,0:T(8,128)(2,1)}, bf16[6,128,256]{2,1,0:T(8,128)(2,1)}, bf16[6,128,256]{2,1,0:T(8,128)(2,1)}, bf16[6,128,256]{2,1,0:T(8...) custom-call(s32[1]{0:T(128)} %bitcast.live_ref, ...), custom_call_target="tpu_custom_call" | custom-call | flops 2415919104 | bytes 28311552 | tf_op jit(solution)/shard_map/backward_tiles/pallas_call | solution.py:148
  130.6 3.9 %collective-permute-start.32 = (bf16[24,128,256]{2,1,0:T(8,128)(2,1)}, bf16[24,128,256]{2,1,0:T(8,128)(2,1)S(1)}, u32[]{:S(2)}, u32[]{:S(2)}) collective-permute-start(bf16[24,128,256]{2,1,0:T(8,128)(2,1)} %get-tuple-element.24), channel_id=1, source_target_pairs={{0,8},{8,0},{1,9},{9,1},{2,10},{10,2},{3,11},{11,3},{4,12},{12,4},... | collective-permute-start | bytes 4718600 | tf_op jit(solution)/shard_map/ppermute | solution.py:39
  134.6 1.0 slice_reduce_fusion
  135.5 0.5 collective-permute-start.42
  136.0 1.7 collective-permute-done.32
  137.7 1.9 add_convert_fusion.4
  139.8 3.2 %collective-permute-start.37 = (bf16[3,128,256]{2,1,0:T(8,128)(2,1)S(1)}, bf16[3,128,256]{2,1,0:T(8,128)(2,1)S(1)}, u32[]{:S(2)}, u32[]{:S(2)}) collective-permute-start(bf16[3,128,256]{2,1,0:T(8,128)(2,1)S(1)} %get-tuple-element.36), channel_id=1, source_target_pairs={{0,112},{16,0},{32,16},{48,32},{64,48},{80,64},{96,80},{112,96},{1... | collective-permute-start | bytes 589832 | tf_op jit(solution)/shard_map/ppermute | solution.py:43
  143.2 5.0 %collective-permute-done.33 = bf16[3,128,256]{2,1,0:T(8,128)(2,1)S(1)} collective-permute-done((bf16[3,128,256]{2,1,0:T(8,128)(2,1)S(1)}, bf16[3,128,256]{2,1,0:T(8,128)(2,1)S(1)}, u32[]{:S(2)}, u32[]{:S(2)}) %collective-permute-start.33) | collective-permute-done | bytes 196640 | tf_op jit(solution)/shard_map/ppermute | solution.py:43
  148.5 3.3 %collective-permute-start.38 = (bf16[6,128,256]{2,1,0:T(8,128)(2,1)S(1)}, bf16[6,128,256]{2,1,0:T(8,128)(2,1)S(1)}, u32[]{:S(2)}, u32[]{:S(2)}) collective-permute-start(bf16[6,128,256]{2,1,0:T(8,128)(2,1)S(1)} %pad_maximum_fusion.1), channel_id=1, source_target_pairs={{0,112},{16,0},{32,16},{48,32},{64,48},{80,64},{96,80},{112,96},{1... | collective-permute-start | bytes 1179656 | tf_op jit(solution)/shard_map/ppermute | solution.py:43
  151.8 1.2 collective-permute-start.43
  152.9 7.2 %collective-permute-done.34 = bf16[6,128,256]{2,1,0:T(8,128)(2,1)S(1)} collective-permute-done((bf16[6,128,256]{2,1,0:T(8,128)(2,1)S(1)}, bf16[6,128,256]{2,1,0:T(8,128)(2,1)S(1)}, u32[]{:S(2)}, u32[]{:S(2)}) %collective-permute-start.34) | collective-permute-done | bytes 393248 | tf_op jit(solution)/shard_map/ppermute | solution.py:43
  160.4 0.9 add_convert_fusion.1
  161.3 3.2 %collective-permute-start.39 = (bf16[6,128,256]{2,1,0:T(8,128)(2,1)}, bf16[6,128,256]{2,1,0:T(8,128)(2,1)S(1)}, u32[]{:S(2)}, u32[]{:S(2)}) collective-permute-start(bf16[6,128,256]{2,1,0:T(8,128)(2,1)} %add_convert_fusion.1), channel_id=1, source_target_pairs={{0,112},{16,0},{32,16},{48,32},{64,48},{80,64},{96,80},{112,96},{1... | collective-permute-start | bytes 1179656 | tf_op jit(solution)/shard_map/ppermute | solution.py:43
  164.5 0.7 tile.4
  165.2 3.4 %all-to-all-start.2 = ((bf16[8,48,256]{2,1,0:T(8,128)(2,1)}), bf16[8,48,256]{2,1,0:T(8,128)(2,1)S(1)}, u32[]{:S(2)}, u32[]{:S(2)}) async-start(bf16[8,48,256]{2,1,0:T(8,128)(2,1)} %tile.4), calls=%async_computation.2 | async-start | bytes 393216 | tf_op jit(solution)/shard_map/all_to_all | solution.py:287
  168.6 3.7 %collective-permute-done.35 = bf16[6,128,256]{2,1,0:T(8,128)(2,1)S(1)} collective-permute-done((bf16[6,128,256]{2,1,0:T(8,128)(2,1)S(1)}, bf16[6,128,256]{2,1,0:T(8,128)(2,1)S(1)}, u32[]{:S(2)}, u32[]{:S(2)}) %collective-permute-start.35) | collective-permute-done | bytes 393248 | tf_op jit(solution)/shard_map/ppermute | solution.py:43
  172.3 0.9 add_convert_fusion.2
  173.2 1.7 collective-permute-done.39
  174.9 2.0 %add_convert_fusion = bf16[6,128,256]{2,1,0:T(8,128)(2,1)} fusion(bf16[6,128,256]{2,1,0:T(8,128)(2,1)S(1)} %collective-permute-done.39, bf16[6,128,256]{2,1,0:T(8,128)(2,1)} %get-tuple-element.25, bf16[24,128,256]{2,1,0:T(8,128)(2,1)} %copy-done), kind=kLoop, calls=%fused_computation.1 | loop fusion | flops 1179648 | bytes 1572864 | tf_op jit(solution)/shard_map/convert_element_type | solution.py:251
  176.9 3.6 %collective-permute-start.40 = (bf16[6,128,256]{2,1,0:T(8,128)(2,1)}, bf16[6,128,256]{2,1,0:T(8,128)(2,1)}, u32[]{:S(2)}, u32[]{:S(2)}) collective-permute-start(bf16[6,128,256]{2,1,0:T(8,128)(2,1)} %add_convert_fusion), channel_id=1, source_target_pairs={{0,112},{16,0},{32,16},{48,32},{64,48},{80,64},{96,80},{112,96},{1... | collective-permute-start | bytes 1179656 | tf_op jit(solution)/shard_map/ppermute | solution.py:43
  180.6 0.7 tile.5
  181.4 7.9 %all-to-all-start.3 = ((f32[8,32,256]{2,1,0:T(8,128)}), f32[8,32,256]{2,1,0:T(8,128)S(1)}, u32[]{:S(2)}, u32[]{:S(2)}) async-start(f32[8,32,256]{2,1,0:T(8,128)} %tile.5), calls=%async_computation.3 | async-start | bytes 524288 | tf_op jit(solution)/shard_map/all_to_all | solution.py:290
  189.3 1.2 convert_add_fusion
  190.7 1.3 slice.117
  191.9 3.5 %all-to-all-done.3 = f32[8,32,256]{2,1,0:T(8,128)S(1)} async-done(((f32[8,32,256]{2,1,0:T(8,128)}), f32[8,32,256]{2,1,0:T(8,128)S(1)}, u32[]{:S(2)}, u32[]{:S(2)}) %all-to-all-start.3) | async-done | bytes 262176 | tf_op jit(solution)/shard_map/all_to_all | solution.py:290
  195.4 2.4 %collective-permute-done.41 = bf16[3,128,256]{2,1,0:T(8,128)(2,1)S(1)} collective-permute-done((bf16[3,128,256]{2,1,0:T(8,128)(2,1)S(1)}, bf16[3,128,256]{2,1,0:T(8,128)(2,1)S(1)}, u32[]{:S(2)}, u32[]{:S(2)}) %collective-permute-start.41) | collective-permute-done | bytes 196640 | tf_op jit(solution)/shard_map/ppermute | solution.py:39
  197.8 0.7 fusion
  198.5 0.7 copy.12
  (140 shorter events, 1.6 us)
Async XLA Ops:
  0.6 8.4 %collective-permute-start = (bf16[3,128,256]{2,1,0:T(8,128)(2,1)}, bf16[3,128,256]{2,1,0:T(8,128)(2,1)S(1)}, u32[]{:S(2)}, u32[]{:S(2)}) collective-permute-start(bf16[3,128,256]{2,1,0:T(8,128)(2,1)} %bitcast.18), channel_id=1, source_target_pairs={{0,128},{128,0},{1,129},{129,1},{2,130},{130,2},{3,131},{131,3},{4... | collective-permute-start | bytes 589832 | tf_op jit(solution)/shard_map/ppermute | solution.py:39
  2.8 12.1 %collective-permute-start.3 = (bf16[3,128,256]{2,1,0:T(8,128)(2,1)}, bf16[3,128,256]{2,1,0:T(8,128)(2,1)S(1)}, u32[]{:S(2)}, u32[]{:S(2)}) collective-permute-start(bf16[3,128,256]{2,1,0:T(8,128)(2,1)} %bitcast.19), channel_id=1, source_target_pairs={{0,16},{16,32},{32,48},{48,64},{64,80},{80,96},{96,112},{112,0},{1... | collective-permute-start | bytes 589832 | tf_op jit(solution)/shard_map/ppermute | solution.py:43
  4.8 10.3 %collective-permute-start.7 = (bf16[3,128,256]{2,1,0:T(8,128)(2,1)}, bf16[3,128,256]{2,1,0:T(8,128)(2,1)S(1)}, u32[]{:S(2)}, u32[]{:S(2)}) collective-permute-start(bf16[3,128,256]{2,1,0:T(8,128)(2,1)} %bitcast.20), channel_id=1, source_target_pairs={{0,112},{16,0},{32,16},{48,32},{64,48},{80,64},{96,80},{112,96},{1... | collective-permute-start | bytes 589832 | tf_op jit(solution)/shard_map/ppermute | solution.py:43
  8.7 9.6 %collective-permute-start.1 = (bf16[3,128,256]{2,1,0:T(8,128)(2,1)}, bf16[3,128,256]{2,1,0:T(8,128)(2,1)S(1)}, u32[]{:S(2)}, u32[]{:S(2)}) collective-permute-start(bf16[3,128,256]{2,1,0:T(8,128)(2,1)} %bitcast.21), channel_id=1, source_target_pairs={{0,8},{8,0},{1,9},{9,1},{2,10},{10,2},{3,11},{11,3},{4,12},{12,4},... | collective-permute-start | bytes 589832 | tf_op jit(solution)/shard_map/ppermute | solution.py:39
  9.1 43.6 %copy-start.6 = (bf16[3,128,256]{2,1,0:T(8,128)(2,1)}, bf16[3,128,256]{2,1,0:T(8,128)(2,1)S(1)}, u32[]{:S(2)}) copy-start(bf16[3,128,256]{2,1,0:T(8,128)(2,1)S(1)} %collective-permute-done.refs_1_) | copy-start | bytes 589828
  9.1 10.6 %collective-permute-start.8 = (bf16[3,128,256]{2,1,0:T(8,128)(2,1)S(1)}, bf16[3,128,256]{2,1,0:T(8,128)(2,1)S(1)}, u32[]{:S(2)}, u32[]{:S(2)}) collective-permute-start(bf16[3,128,256]{2,1,0:T(8,128)(2,1)S(1)} %collective-permute-done.refs_1_), channel_id=1, source_target_pairs={{0,112},{16,0},{32,16},{48,32},{64,48},{80,64},{96,80},{112,96},{1... | collective-permute-start | bytes 589832 | tf_op jit(solution)/shard_map/ppermute | solution.py:43
  14.9 8.8 %collective-permute-start.4 = (bf16[3,128,256]{2,1,0:T(8,128)(2,1)S(1)}, bf16[3,128,256]{2,1,0:T(8,128)(2,1)S(1)}, u32[]{:S(2)}, u32[]{:S(2)}) collective-permute-start(bf16[3,128,256]{2,1,0:T(8,128)(2,1)S(1)} %collective-permute-done.refs_1_), channel_id=1, source_target_pairs={{0,16},{16,32},{32,48},{48,64},{64,80},{80,96},{96,112},{112,0},{1... | collective-permute-start | bytes 589832 | tf_op jit(solution)/shard_map/ppermute | solution.py:43
  14.9 37.8 %copy-start.7 = (bf16[3,128,256]{2,1,0:T(8,128)(2,1)}, bf16[3,128,256]{2,1,0:T(8,128)(2,1)S(1)}, u32[]{:S(2)}) copy-start(bf16[3,128,256]{2,1,0:T(8,128)(2,1)S(1)} %collective-permute-done.3.refs_4_) | copy-start | bytes 589828
  14.9 10.9 %collective-permute-start.11 = (bf16[3,128,256]{2,1,0:T(8,128)(2,1)S(1)}, bf16[3,128,256]{2,1,0:T(8,128)(2,1)S(1)}, u32[]{:S(2)}, u32[]{:S(2)}) collective-permute-start(bf16[3,128,256]{2,1,0:T(8,128)(2,1)S(1)} %collective-permute-done.3.refs_4_), channel_id=1, source_target_pairs={{0,16},{16,32},{32,48},{48,64},{64,80},{80,96},{96,112},{112,0},{1... | collective-permute-start | bytes 589832 | tf_op jit(solution)/shard_map/ppermute | solution.py:43
  15.0 37.7 %copy-start.8 = (bf16[3,128,256]{2,1,0:T(8,128)(2,1)}, bf16[3,128,256]{2,1,0:T(8,128)(2,1)S(1)}, u32[]{:S(2)}) copy-start(bf16[3,128,256]{2,1,0:T(8,128)(2,1)S(1)} %collective-permute-done.7.refs_8_) | copy-start | bytes 589828
  15.1 10.8 %collective-permute-start.15 = (bf16[3,128,256]{2,1,0:T(8,128)(2,1)S(1)}, bf16[3,128,256]{2,1,0:T(8,128)(2,1)S(1)}, u32[]{:S(2)}, u32[]{:S(2)}) collective-permute-start(bf16[3,128,256]{2,1,0:T(8,128)(2,1)S(1)} %collective-permute-done.7.refs_8_), channel_id=1, source_target_pairs={{0,112},{16,0},{32,16},{48,32},{64,48},{80,64},{96,80},{112,96},{1... | collective-permute-start | bytes 589832 | tf_op jit(solution)/shard_map/ppermute | solution.py:43
  18.3 34.4 %copy-start.9 = (bf16[3,128,256]{2,1,0:T(8,128)(2,1)}, bf16[3,128,256]{2,1,0:T(8,128)(2,1)S(1)}, u32[]{:S(2)}) copy-start(bf16[3,128,256]{2,1,0:T(8,128)(2,1)S(1)} %collective-permute-done.1.refs_2_) | copy-start | bytes 589828
  18.3 9.6 %collective-permute-start.2 = (bf16[3,128,256]{2,1,0:T(8,128)(2,1)S(1)}, bf16[3,128,256]{2,1,0:T(8,128)(2,1)S(1)}, u32[]{:S(2)}, u32[]{:S(2)}) collective-permute-start(bf16[3,128,256]{2,1,0:T(8,128)(2,1)S(1)} %collective-permute-done.refs_1_), channel_id=1, source_target_pairs={{0,8},{8,0},{1,9},{9,1},{2,10},{10,2},{3,11},{11,3},{4,12},{12,4},... | collective-permute-start | bytes 589832 | tf_op jit(solution)/shard_map/ppermute | solution.py:39
  19.7 33.0 %copy-start.10 = (bf16[3,128,256]{2,1,0:T(8,128)(2,1)}, bf16[3,128,256]{2,1,0:T(8,128)(2,1)S(1)}, u32[]{:S(2)}) copy-start(bf16[3,128,256]{2,1,0:T(8,128)(2,1)S(1)} %collective-permute-done.8.refs_9_) | copy-start | bytes 589828
  19.7 8.3 %collective-permute-start.5 = (bf16[3,128,256]{2,1,0:T(8,128)(2,1)S(1)}, bf16[3,128,256]{2,1,0:T(8,128)(2,1)S(1)}, u32[]{:S(2)}, u32[]{:S(2)}) collective-permute-start(bf16[3,128,256]{2,1,0:T(8,128)(2,1)S(1)} %collective-permute-done.3.refs_4_), channel_id=1, source_target_pairs={{0,8},{8,0},{1,9},{9,1},{2,10},{10,2},{3,11},{11,3},{4,12},{12,4},... | collective-permute-start | bytes 589832 | tf_op jit(solution)/shard_map/ppermute | solution.py:39
  23.7 29.0 %copy-start.11 = (bf16[3,128,256]{2,1,0:T(8,128)(2,1)}, bf16[3,128,256]{2,1,0:T(8,128)(2,1)S(1)}, u32[]{:S(2)}) copy-start(bf16[3,128,256]{2,1,0:T(8,128)(2,1)S(1)} %collective-permute-done.4.refs_5_) | copy-start | bytes 589828
  23.7 7.4 %collective-permute-start.9 = (bf16[3,128,256]{2,1,0:T(8,128)(2,1)S(1)}, bf16[3,128,256]{2,1,0:T(8,128)(2,1)S(1)}, u32[]{:S(2)}, u32[]{:S(2)}) collective-permute-start(bf16[3,128,256]{2,1,0:T(8,128)(2,1)S(1)} %collective-permute-done.7.refs_8_), channel_id=1, source_target_pairs={{0,8},{8,0},{1,9},{9,1},{2,10},{10,2},{3,11},{11,3},{4,12},{12,4},... | collective-permute-start | bytes 589832 | tf_op jit(solution)/shard_map/ppermute | solution.py:39
  25.8 26.9 %copy-start.12 = (bf16[3,128,256]{2,1,0:T(8,128)(2,1)}, bf16[3,128,256]{2,1,0:T(8,128)(2,1)S(1)}, u32[]{:S(2)}) copy-start(bf16[3,128,256]{2,1,0:T(8,128)(2,1)S(1)} %collective-permute-done.11.refs_12_) | copy-start | bytes 589828
  25.8 7.3 %collective-permute-start.16 = (bf16[3,128,256]{2,1,0:T(8,128)(2,1)S(1)}, bf16[3,128,256]{2,1,0:T(8,128)(2,1)S(1)}, u32[]{:S(2)}, u32[]{:S(2)}) collective-permute-start(bf16[3,128,256]{2,1,0:T(8,128)(2,1)S(1)} %collective-permute-done.8.refs_9_), channel_id=1, source_target_pairs={{0,112},{16,0},{32,16},{48,32},{64,48},{80,64},{96,80},{112,96},{1... | collective-permute-start | bytes 589832 | tf_op jit(solution)/shard_map/ppermute | solution.py:43
  25.9 26.9 %copy-start.13 = (bf16[3,128,256]{2,1,0:T(8,128)(2,1)}, bf16[3,128,256]{2,1,0:T(8,128)(2,1)S(1)}, u32[]{:S(2)}) copy-start(bf16[3,128,256]{2,1,0:T(8,128)(2,1)S(1)} %collective-permute-done.15.refs_16_) | copy-start | bytes 589828
  25.9 8.6 %collective-permute-start.12 = (bf16[3,128,256]{2,1,0:T(8,128)(2,1)S(1)}, bf16[3,128,256]{2,1,0:T(8,128)(2,1)S(1)}, u32[]{:S(2)}, u32[]{:S(2)}) collective-permute-start(bf16[3,128,256]{2,1,0:T(8,128)(2,1)S(1)} %collective-permute-done.4.refs_5_), channel_id=1, source_target_pairs={{0,16},{16,32},{32,48},{48,64},{64,80},{80,96},{96,112},{112,0},{1... | collective-permute-start | bytes 589832 | tf_op jit(solution)/shard_map/ppermute | solution.py:43
  27.9 24.9 %copy-start.14 = (bf16[3,128,256]{2,1,0:T(8,128)(2,1)}, bf16[3,128,256]{2,1,0:T(8,128)(2,1)S(1)}, u32[]{:S(2)}) copy-start(bf16[3,128,256]{2,1,0:T(8,128)(2,1)S(1)} %collective-permute-done.2.refs_3_) | copy-start | bytes 589828
  27.9 8.7 %collective-permute-start.19 = (bf16[3,128,256]{2,1,0:T(8,128)(2,1)S(1)}, bf16[3,128,256]{2,1,0:T(8,128)(2,1)S(1)}, u32[]{:S(2)}, u32[]{:S(2)}) collective-permute-start(bf16[3,128,256]{2,1,0:T(8,128)(2,1)S(1)} %collective-permute-done.11.refs_12_), channel_id=1, source_target_pairs={{0,16},{16,32},{32,48},{48,64},{64,80},{80,96},{96,112},{112,0},{1... | collective-permute-start | bytes 589832 | tf_op jit(solution)/shard_map/ppermute | solution.py:43
  28.0 24.8 %copy-start.15 = (bf16[3,128,256]{2,1,0:T(8,128)(2,1)}, bf16[3,128,256]{2,1,0:T(8,128)(2,1)S(1)}, u32[]{:S(2)}) copy-start(bf16[3,128,256]{2,1,0:T(8,128)(2,1)S(1)} %collective-permute-done.5.refs_6_) | copy-start | bytes 589828
  28.0 8.6 %collective-permute-start.23 = (bf16[3,128,256]{2,1,0:T(8,128)(2,1)S(1)}, bf16[3,128,256]{2,1,0:T(8,128)(2,1)S(1)}, u32[]{:S(2)}, u32[]{:S(2)}) collective-permute-start(bf16[3,128,256]{2,1,0:T(8,128)(2,1)S(1)} %collective-permute-done.15.refs_16_), channel_id=1, source_target_pairs={{0,112},{16,0},{32,16},{48,32},{64,48},{80,64},{96,80},{112,96},{1... | collective-permute-start | bytes 589832 | tf_op jit(solution)/shard_map/ppermute | solution.py:43
  31.1 21.7 %copy-start.16 = (bf16[3,128,256]{2,1,0:T(8,128)(2,1)}, bf16[3,128,256]{2,1,0:T(8,128)(2,1)S(1)}, u32[]{:S(2)}) copy-start(bf16[3,128,256]{2,1,0:T(8,128)(2,1)S(1)} %collective-permute-done.9.refs_10_) | copy-start | bytes 589828
  31.1 6.9 %collective-permute-start.10 = (bf16[3,128,256]{2,1,0:T(8,128)(2,1)S(1)}, bf16[3,128,256]{2,1,0:T(8,128)(2,1)S(1)}, u32[]{:S(2)}, u32[]{:S(2)}) collective-permute-start(bf16[3,128,256]{2,1,0:T(8,128)(2,1)S(1)} %collective-permute-done.8.refs_9_), channel_id=1, source_target_pairs={{0,8},{8,0},{1,9},{9,1},{2,10},{10,2},{3,11},{11,3},{4,12},{12,4},... | collective-permute-start | bytes 589832 | tf_op jit(solution)/shard_map/ppermute | solution.py:39
  33.2 19.6 %copy-start.17 = (bf16[3,128,256]{2,1,0:T(8,128)(2,1)}, bf16[3,128,256]{2,1,0:T(8,128)(2,1)S(1)}, u32[]{:S(2)}) copy-start(bf16[3,128,256]{2,1,0:T(8,128)(2,1)S(1)} %collective-permute-done.16.refs_17_) | copy-start | bytes 589828
  33.2 7.6 %collective-permute-start.6 = (bf16[3,128,256]{2,1,0:T(8,128)(2,1)S(1)}, bf16[3,128,256]{2,1,0:T(8,128)(2,1)S(1)}, u32[]{:S(2)}, u32[]{:S(2)}) collective-permute-start(bf16[3,128,256]{2,1,0:T(8,128)(2,1)S(1)} %collective-permute-done.4.refs_5_), channel_id=1, source_target_pairs={{0,8},{8,0},{1,9},{9,1},{2,10},{10,2},{3,11},{11,3},{4,12},{12,4},... | collective-permute-start | bytes 589832 | tf_op jit(solution)/shard_map/ppermute | solution.py:39
  34.5 18.3 %copy-start.18 = (bf16[3,128,256]{2,1,0:T(8,128)(2,1)}, bf16[3,128,256]{2,1,0:T(8,128)(2,1)S(1)}, u32[]{:S(2)}) copy-start(bf16[3,128,256]{2,1,0:T(8,128)(2,1)S(1)} %collective-permute-done.12.refs_13_) | copy-start | bytes 589828
  34.5 6.3 %collective-permute-start.13 = (bf16[3,128,256]{2,1,0:T(8,128)(2,1)S(1)}, bf16[3,128,256]{2,1,0:T(8,128)(2,1)S(1)}, u32[]{:S(2)}, u32[]{:S(2)}) collective-permute-start(bf16[3,128,256]{2,1,0:T(8,128)(2,1)S(1)} %collective-permute-done.11.refs_12_), channel_id=1, source_target_pairs={{0,8},{8,0},{1,9},{9,1},{2,10},{10,2},{3,11},{11,3},{4,12},{12,4},... | collective-permute-start | bytes 589832 | tf_op jit(solution)/shard_map/ppermute | solution.py:39
  36.6 16.2 %copy-start.19 = (bf16[3,128,256]{2,1,0:T(8,128)(2,1)}, bf16[3,128,256]{2,1,0:T(8,128)(2,1)S(1)}, u32[]{:S(2)}) copy-start(bf16[3,128,256]{2,1,0:T(8,128)(2,1)S(1)} %collective-permute-done.19.refs_20_) | copy-start | bytes 589828
  36.6 4.7 %collective-permute-start.17 = (bf16[3,128,256]{2,1,0:T(8,128)(2,1)S(1)}, bf16[3,128,256]{2,1,0:T(8,128)(2,1)S(1)}, u32[]{:S(2)}, u32[]{:S(2)}) collective-permute-start(bf16[3,128,256]{2,1,0:T(8,128)(2,1)S(1)} %collective-permute-done.15.refs_16_), channel_id=1, source_target_pairs={{0,8},{8,0},{1,9},{9,1},{2,10},{10,2},{3,11},{11,3},{4,12},{12,4},... | collective-permute-start | bytes 589832 | tf_op jit(solution)/shard_map/ppermute | solution.py:39
  36.6 16.2 %copy-start.20 = (bf16[3,128,256]{2,1,0:T(8,128)(2,1)}, bf16[3,128,256]{2,1,0:T(8,128)(2,1)S(1)}, u32[]{:S(2)}) copy-start(bf16[3,128,256]{2,1,0:T(8,128)(2,1)S(1)} %collective-permute-done.23.refs_24_) | copy-start | bytes 589828
  36.6 7.3 %collective-permute-start.24 = (bf16[3,128,256]{2,1,0:T(8,128)(2,1)S(1)}, bf16[3,128,256]{2,1,0:T(8,128)(2,1)S(1)}, u32[]{:S(2)}, u32[]{:S(2)}) collective-permute-start(bf16[3,128,256]{2,1,0:T(8,128)(2,1)S(1)} %collective-permute-done.16.refs_17_), channel_id=1, source_target_pairs={{0,112},{16,0},{32,16},{48,32},{64,48},{80,64},{96,80},{112,96},{1... | collective-permute-start | bytes 589832 | tf_op jit(solution)/shard_map/ppermute | solution.py:43
  38.0 7.2 %collective-permute-start.20 = (bf16[3,128,256]{2,1,0:T(8,128)(2,1)S(1)}, bf16[3,128,256]{2,1,0:T(8,128)(2,1)S(1)}, u32[]{:S(2)}, u32[]{:S(2)}) collective-permute-start(bf16[3,128,256]{2,1,0:T(8,128)(2,1)S(1)} %collective-permute-done.12.refs_13_), channel_id=1, source_target_pairs={{0,16},{16,32},{32,48},{48,64},{64,80},{80,96},{96,112},{112,0},{1... | collective-permute-start | bytes 589832 | tf_op jit(solution)/shard_map/ppermute | solution.py:43
  40.8 8.7 %collective-permute-start.14 = (bf16[3,128,256]{2,1,0:T(8,128)(2,1)S(1)}, bf16[3,128,256]{2,1,0:T(8,128)(2,1)S(1)}, u32[]{:S(2)}, u32[]{:S(2)}) collective-permute-start(bf16[3,128,256]{2,1,0:T(8,128)(2,1)S(1)} %collective-permute-done.12.refs_13_), channel_id=1, source_target_pairs={{0,8},{8,0},{1,9},{9,1},{2,10},{10,2},{3,11},{11,3},{4,12},{12,4},... | collective-permute-start | bytes 589832 | tf_op jit(solution)/shard_map/ppermute | solution.py:39
  40.8 9.2 %collective-permute-start.18 = (bf16[3,128,256]{2,1,0:T(8,128)(2,1)S(1)}, bf16[3,128,256]{2,1,0:T(8,128)(2,1)S(1)}, u32[]{:S(2)}, u32[]{:S(2)}) collective-permute-start(bf16[3,128,256]{2,1,0:T(8,128)(2,1)S(1)} %collective-permute-done.16.refs_17_), channel_id=1, source_target_pairs={{0,8},{8,0},{1,9},{9,1},{2,10},{10,2},{3,11},{11,3},{4,12},{12,4},... | collective-permute-start | bytes 589832 | tf_op jit(solution)/shard_map/ppermute | solution.py:39
  41.3 8.2 %collective-permute-start.27 = (bf16[3,128,256]{2,1,0:T(8,128)(2,1)S(1)}, bf16[3,128,256]{2,1,0:T(8,128)(2,1)S(1)}, u32[]{:S(2)}, u32[]{:S(2)}) collective-permute-start(bf16[3,128,256]{2,1,0:T(8,128)(2,1)S(1)} %collective-permute-done.19.refs_20_), channel_id=1, source_target_pairs={{0,16},{16,32},{32,48},{48,64},{64,80},{80,96},{96,112},{112,0},{1... | collective-permute-start | bytes 589832 | tf_op jit(solution)/shard_map/ppermute | solution.py:43
  43.9 6.1 %collective-permute-start.21 = (bf16[3,128,256]{2,1,0:T(8,128)(2,1)S(1)}, bf16[3,128,256]{2,1,0:T(8,128)(2,1)S(1)}, u32[]{:S(2)}, u32[]{:S(2)}) collective-permute-start(bf16[3,128,256]{2,1,0:T(8,128)(2,1)S(1)} %collective-permute-done.19.refs_20_), channel_id=1, source_target_pairs={{0,8},{8,0},{1,9},{9,1},{2,10},{10,2},{3,11},{11,3},{4,12},{12,4},... | collective-permute-start | bytes 589832 | tf_op jit(solution)/shard_map/ppermute | solution.py:39
  45.2 6.0 %collective-permute-start.28 = (bf16[3,128,256]{2,1,0:T(8,128)(2,1)S(1)}, bf16[3,128,256]{2,1,0:T(8,128)(2,1)S(1)}, u32[]{:S(2)}, u32[]{:S(2)}) collective-permute-start(bf16[3,128,256]{2,1,0:T(8,128)(2,1)S(1)} %collective-permute-done.24.refs_25_), channel_id=1, source_target_pairs={{0,112},{16,0},{32,16},{48,32},{64,48},{80,64},{96,80},{112,96},{1... | collective-permute-start | bytes 589832 | tf_op jit(solution)/shard_map/ppermute | solution.py:43
  49.4 2.5 %collective-permute-start.25 = (bf16[3,128,256]{2,1,0:T(8,128)(2,1)S(1)}, bf16[3,128,256]{2,1,0:T(8,128)(2,1)S(1)}, u32[]{:S(2)}, u32[]{:S(2)}) collective-permute-start(bf16[3,128,256]{2,1,0:T(8,128)(2,1)S(1)} %collective-permute-done.23.refs_24_), channel_id=1, source_target_pairs={{0,8},{8,0},{1,9},{9,1},{2,10},{10,2},{3,11},{11,3},{4,12},{12,4},... | collective-permute-start | bytes 589832 | tf_op jit(solution)/shard_map/ppermute | solution.py:39
  49.5 2.5 %collective-permute-start.26 = (bf16[3,128,256]{2,1,0:T(8,128)(2,1)S(1)}, bf16[3,128,256]{2,1,0:T(8,128)(2,1)S(1)}, u32[]{:S(2)}, u32[]{:S(2)}) collective-permute-start(bf16[3,128,256]{2,1,0:T(8,128)(2,1)S(1)} %collective-permute-done.24.refs_25_), channel_id=1, source_target_pairs={{0,8},{8,0},{1,9},{9,1},{2,10},{10,2},{3,11},{11,3},{4,12},{12,4},... | collective-permute-start | bytes 589832 | tf_op jit(solution)/shard_map/ppermute | solution.py:39
  50.0 2.0 collective-permute-start.22
  50.1 1.9 collective-permute-start.29
  51.3 1.4 collective-permute-start.30
  130.6 7.2 %collective-permute-start.32 = (bf16[24,128,256]{2,1,0:T(8,128)(2,1)}, bf16[24,128,256]{2,1,0:T(8,128)(2,1)S(1)}, u32[]{:S(2)}, u32[]{:S(2)}) collective-permute-start(bf16[24,128,256]{2,1,0:T(8,128)(2,1)} %get-tuple-element.24), channel_id=1, source_target_pairs={{0,8},{8,0},{1,9},{9,1},{2,10},{10,2},{3,11},{11,3},{4,12},{12,4},... | collective-permute-start | bytes 4718600 | tf_op jit(solution)/shard_map/ppermute | solution.py:39
  134.5 8.5 %collective-permute-start.31 = (bf16[24,128,256]{2,1,0:T(8,128)(2,1)}, bf16[24,128,256]{2,1,0:T(8,128)(2,1)S(1)}, u32[]{:S(2)}, u32[]{:S(2)}) collective-permute-start(bf16[24,128,256]{2,1,0:T(8,128)(2,1)} %get-tuple-element.19), channel_id=1, source_target_pairs={{0,8},{8,0},{1,9},{9,1},{2,10},{10,2},{3,11},{11,3},{4,12},{12,4},... | collective-permute-start | bytes 4718600 | tf_op jit(solution)/shard_map/ppermute | solution.py:39
  135.5 16.2 %collective-permute-start.42 = (bf16[48,256]{1,0:T(8,128)(2,1)S(1)}, bf16[48,256]{1,0:T(8,128)(2,1)S(1)}, u32[]{:S(2)}, u32[]{:S(2)}) collective-permute-start(bf16[48,256]{1,0:T(8,128)(2,1)S(1)} %slice_reduce_fusion), channel_id=1, source_target_pairs={{0,8},{8,0},{1,9},{9,1},{2,10},{10,2},{3,11},{11,3},{4,12},{12,4},... | collective-permute-start | bytes 73736 | tf_op jit(solution)/shard_map/ppermute | solution.py:39
  137.7 22.6 %copy-start = (bf16[24,128,256]{2,1,0:T(8,128)(2,1)}, bf16[24,128,256]{2,1,0:T(8,128)(2,1)S(1)}, u32[]{:S(2)}) copy-start(bf16[24,128,256]{2,1,0:T(8,128)(2,1)S(1)} %collective-permute-done.32) | copy-start | bytes 4718596
  139.7 8.5 %collective-permute-start.33 = (bf16[3,128,256]{2,1,0:T(8,128)(2,1)S(1)}, bf16[3,128,256]{2,1,0:T(8,128)(2,1)S(1)}, u32[]{:S(2)}, u32[]{:S(2)}) collective-permute-start(bf16[3,128,256]{2,1,0:T(8,128)(2,1)S(1)} %get-tuple-element.35), channel_id=1, source_target_pairs={{0,16},{16,32},{32,48},{48,64},{64,80},{80,96},{96,112},{112,0},{1... | collective-permute-start | bytes 589832 | tf_op jit(solution)/shard_map/ppermute | solution.py:43
  139.8 8.6 %collective-permute-start.37 = (bf16[3,128,256]{2,1,0:T(8,128)(2,1)S(1)}, bf16[3,128,256]{2,1,0:T(8,128)(2,1)S(1)}, u32[]{:S(2)}, u32[]{:S(2)}) collective-permute-start(bf16[3,128,256]{2,1,0:T(8,128)(2,1)S(1)} %get-tuple-element.36), channel_id=1, source_target_pairs={{0,112},{16,0},{32,16},{48,32},{64,48},{80,64},{96,80},{112,96},{1... | collective-permute-start | bytes 589832 | tf_op jit(solution)/shard_map/ppermute | solution.py:43
  143.2 17.0 %copy-start.4 = (bf16[6,128,256]{2,1,0:T(8,128)(2,1)S(1)}, bf16[6,128,256]{2,1,0:T(8,128)(2,1)}, u32[]{:S(2)}) copy-start(bf16[6,128,256]{2,1,0:T(8,128)(2,1)} %get-tuple-element.21) | copy-start | bytes 1179652
  148.3 11.9 %collective-permute-start.34 = (bf16[6,128,256]{2,1,0:T(8,128)(2,1)S(1)}, bf16[6,128,256]{2,1,0:T(8,128)(2,1)S(1)}, u32[]{:S(2)}, u32[]{:S(2)}) collective-permute-start(bf16[6,128,256]{2,1,0:T(8,128)(2,1)S(1)} %pad_maximum_fusion), channel_id=1, source_target_pairs={{0,16},{16,32},{32,48},{48,64},{64,80},{80,96},{96,112},{112,0},{1... | collective-permute-start | bytes 1179656 | tf_op jit(solution)/shard_map/ppermute | solution.py:43
  148.5 11.9 %collective-permute-start.38 = (bf16[6,128,256]{2,1,0:T(8,128)(2,1)S(1)}, bf16[6,128,256]{2,1,0:T(8,128)(2,1)S(1)}, u32[]{:S(2)}, u32[]{:S(2)}) collective-permute-start(bf16[6,128,256]{2,1,0:T(8,128)(2,1)S(1)} %pad_maximum_fusion.1), channel_id=1, source_target_pairs={{0,112},{16,0},{32,16},{48,32},{64,48},{80,64},{96,80},{112,96},{1... | collective-permute-start | bytes 1179656 | tf_op jit(solution)/shard_map/ppermute | solution.py:43
  151.8 12.7 %collective-permute-start.43 = (bf16[48,256]{1,0:T(8,128)(2,1)S(1)}, bf16[48,256]{1,0:T(8,128)(2,1)S(1)}, u32[]{:S(2)}, u32[]{:S(2)}) collective-permute-start(bf16[48,256]{1,0:T(8,128)(2,1)S(1)} %add_convert_fusion.5), channel_id=1, source_target_pairs={{0,128},{128,0},{1,129},{129,1},{2,130},{130,2},{3,131},{131,3},{4... | collective-permute-start | bytes 73736 | tf_op jit(solution)/shard_map/ppermute | solution.py:39
  160.3 12.0 %collective-permute-start.35 = (bf16[6,128,256]{2,1,0:T(8,128)(2,1)S(1)}, bf16[6,128,256]{2,1,0:T(8,128)(2,1)S(1)}, u32[]{:S(2)}, u32[]{:S(2)}) collective-permute-start(bf16[6,128,256]{2,1,0:T(8,128)(2,1)S(1)} %add_convert_fusion.3), channel_id=1, source_target_pairs={{0,16},{16,32},{32,48},{48,64},{64,80},{80,96},{96,112},{112,0},{1... | collective-permute-start | bytes 1179656 | tf_op jit(solution)/shard_map/ppermute | solution.py:43
  161.3 13.6 %collective-permute-start.39 = (bf16[6,128,256]{2,1,0:T(8,128)(2,1)}, bf16[6,128,256]{2,1,0:T(8,128)(2,1)S(1)}, u32[]{:S(2)}, u32[]{:S(2)}) collective-permute-start(bf16[6,128,256]{2,1,0:T(8,128)(2,1)} %add_convert_fusion.1), channel_id=1, source_target_pairs={{0,112},{16,0},{32,16},{48,32},{64,48},{80,64},{96,80},{112,96},{1... | collective-permute-start | bytes 1179656 | tf_op jit(solution)/shard_map/ppermute | solution.py:43
  165.2 15.4 %all-to-all-start.2 = ((bf16[8,48,256]{2,1,0:T(8,128)(2,1)}), bf16[8,48,256]{2,1,0:T(8,128)(2,1)S(1)}, u32[]{:S(2)}, u32[]{:S(2)}) async-start(bf16[8,48,256]{2,1,0:T(8,128)(2,1)} %tile.4), calls=%async_computation.2 | async-start | bytes 393216 | tf_op jit(solution)/shard_map/all_to_all | solution.py:287
  173.2 16.1 %copy-start.1 = (bf16[6,128,256]{2,1,0:T(8,128)(2,1)S(1)}, bf16[6,128,256]{2,1,0:T(8,128)(2,1)}, u32[]{:S(2)}) copy-start(bf16[6,128,256]{2,1,0:T(8,128)(2,1)} %get-tuple-element.18) | copy-start | bytes 1179652
  173.2 16.1 %collective-permute-start.36 = (bf16[6,128,256]{2,1,0:T(8,128)(2,1)}, bf16[6,128,256]{2,1,0:T(8,128)(2,1)S(1)}, u32[]{:S(2)}, u32[]{:S(2)}) collective-permute-start(bf16[6,128,256]{2,1,0:T(8,128)(2,1)} %add_convert_fusion.2), channel_id=1, source_target_pairs={{0,16},{16,32},{32,48},{48,64},{64,80},{80,96},{96,112},{112,0},{1... | collective-permute-start | bytes 1179656 | tf_op jit(solution)/shard_map/ppermute | solution.py:43
  176.9 12.4 %collective-permute-start.40 = (bf16[6,128,256]{2,1,0:T(8,128)(2,1)}, bf16[6,128,256]{2,1,0:T(8,128)(2,1)}, u32[]{:S(2)}, u32[]{:S(2)}) collective-permute-start(bf16[6,128,256]{2,1,0:T(8,128)(2,1)} %add_convert_fusion), channel_id=1, source_target_pairs={{0,112},{16,0},{32,16},{48,32},{64,48},{80,64},{96,80},{112,96},{1... | collective-permute-start | bytes 1179656 | tf_op jit(solution)/shard_map/ppermute | solution.py:43
  181.4 14.1 %all-to-all-start.3 = ((f32[8,32,256]{2,1,0:T(8,128)}), f32[8,32,256]{2,1,0:T(8,128)S(1)}, u32[]{:S(2)}, u32[]{:S(2)}) async-start(f32[8,32,256]{2,1,0:T(8,128)} %tile.5), calls=%async_computation.3 | async-start | bytes 524288 | tf_op jit(solution)/shard_map/all_to_all | solution.py:290
  190.6 7.3 %collective-permute-start.41 = (bf16[3,128,256]{2,1,0:T(8,128)(2,1)S(1)}, bf16[3,128,256]{2,1,0:T(8,128)(2,1)S(1)}, u32[]{:S(2)}, u32[]{:S(2)}) collective-permute-start(bf16[3,128,256]{2,1,0:T(8,128)(2,1)S(1)} %slice.143), channel_id=1, source_target_pairs={{0,128},{128,0},{1,129},{129,1},{2,130},{130,2},{3,131},{131,3},{4... | collective-permute-start | bytes 589832 | tf_op jit(solution)/shard_map/ppermute | solution.py:39
  (20 other events, 124.6 us)
